TPU v7x, 32 devices: a whole 2x2x4 slice. The times are simulated.
32 devices in a mesh: front: 4 (over z), helper: 8 (over y, x, core).
Axes of the slice: x: 2, y: 2, z: 4, core: 2. Of those that a mesh axis runs over, the one named last changes fastest.
Arguments:
- front: float32 [4, 4096, 4096], P('front', 'helper')
- row_list: int32 [4, 4096], replicated, may hold values from 0 to 4095, as said below
- child_map: int32 [4, 3840], replicated, may hold values from 0 to 8191, as said below
- parent: float32 [8192, 8192], P(('front', 'helper')), may hold values from -6 to 6
Outputs:
- factors: float32 [4, 4096, 4096], P('front', 'helper')
- assembled: float32 [8192, 8192], P(('front', 'helper'))
Inputs may be any that keep to these rules, and one draw needn't show every extreme that they name: Each row of row_list is a permutation; stored rows h * 512 to (h + 1) * 512 - 1 of a front lie on helper h. Of the 256 rows of any panel, one helper holds at most 48, and some helper holds exactly 48 in every panel. The leading 256 x 256 block of every front is well conditioned without pivoting: its diagonal exceeds 2.5 sqrt(256) times the row's spread. `child_map`: distinct within a front. Parent row r lies on device r // 256 of front+helper. Of the contribution rows on one device, at most 16 go to one device's parent rows, and exactly 16 go to some device.
All inputs are finite; a program needn't handle non-finite values.
Results may differ from a plain program's by a relative error of at most 0.0001.
Values sent between devices are 32-bit elements; how exact they have to be, the bound alone decides.
A program may use at most 128 MiB of HBM per device.

v0:
```python
import jax
import jax.numpy as jnp
from jax import lax
from jax.sharding import PartitionSpec as P

PANEL = 256
PIVOTS = 256


def product(left, right):
    return jnp.dot(left, right, precision=lax.Precision.HIGHEST, preferred_element_type=jnp.float32)


def small_inverse(matrix):
    extent = matrix.shape[0]
    augmented = jnp.concatenate([matrix, jnp.eye(extent, dtype=matrix.dtype)], axis=1)
    for column in range(extent):
        pivot_row = augmented[column] / augmented[column, column]
        augmented = augmented - augmented[:, column : column + 1] * pivot_row[None, :]
        augmented = augmented.at[column].set(pivot_row)
    return augmented[:, extent:]


def block_inverse(matrix):
    extent = matrix.shape[0]
    if extent <= 32:
        return small_inverse(matrix)
    middle = extent // 2
    upper_left = matrix[:middle, :middle]
    upper_right = matrix[:middle, middle:]
    lower_left = matrix[middle:, :middle]
    lower_right = matrix[middle:, middle:]
    inverse_left = block_inverse(upper_left)
    coupled = product(inverse_left, upper_right)
    schur_part = lower_right - product(lower_left, coupled)
    inverse_schur = block_inverse(schur_part)
    left_factor = product(lower_left, inverse_left)
    top_right = -product(coupled, inverse_schur)
    bottom_left = -product(inverse_schur, left_factor)
    top_left = inverse_left - product(top_right, left_factor)
    upper_half = jnp.concatenate([top_left, top_right], axis=1)
    lower_half = jnp.concatenate([bottom_left, inverse_schur], axis=1)
    return jnp.concatenate([upper_half, lower_half], axis=0)


def local(front, row_list, child_map, parent):
    front_rows = front[0]
    row_count = front_rows.shape[0]
    helpers = lax.axis_size("helper")
    fronts = lax.axis_size("front")
    devices_all = helpers * fronts
    my_front = lax.axis_index("front")
    my_helper = lax.axis_index("helper")
    front_order = jnp.take(row_list, my_front, axis=0)
    own_ids = lax.dynamic_slice_in_dim(front_order, my_helper * row_count, row_count)
    local_iota = jnp.arange(row_count, dtype=jnp.int32)
    panel_iota = jnp.arange(PANEL, dtype=jnp.int32)
    end_col = PANEL
    trailing = front_rows
    wanted = own_ids[None, :] == (0 + panel_iota)[:, None]
    position = jnp.sum(jnp.where(wanted, local_iota[None, :], 0), axis=1)
    present = jnp.any(wanted, axis=1)
    picked = jnp.where(present[:, None], jnp.take(trailing, position, axis=0), 0.0)
    panel_rows = lax.psum(picked, "helper")
    inverse = block_inverse(panel_rows[:, :PANEL])
    active = (own_ids >= end_col)[:, None]
    current = front_rows[:, 0:end_col]
    lower_part = jnp.where(active, product(current, inverse), 0.0)
    front_rows = front_rows.at[:, 0:end_col].set(jnp.where(active, lower_part, current))
    front_rows = front_rows.at[:, end_col:].add(-product(lower_part, panel_rows[:, PANEL:]))
    parent_rows = parent.shape[0]
    parent_width = parent.shape[1]
    cb_width = front_rows.shape[1] - PIVOTS
    cap_rows = (row_count + devices_all - 1) // devices_all
    device_iota = jnp.arange(devices_all, dtype=jnp.int32)
    own_map = jnp.take(child_map, my_front, axis=0)
    own_cb = own_ids >= PIVOTS
    own_target = jnp.take(own_map, jnp.clip(own_ids - PIVOTS, 0, cb_width - 1))
    owner = jnp.where(own_cb, own_target // parent_rows, devices_all)
    dest_match = owner[:, None] == device_iota[None, :]
    dest_rank = jnp.sum(
        jnp.where(dest_match, jnp.cumsum(dest_match.astype(jnp.int32), axis=0) - 1, 0), axis=1
    )
    outgoing = jnp.zeros((devices_all, cap_rows, cb_width), jnp.float32)
    outgoing = outgoing.at[owner, dest_rank].set(front_rows[:, PIVOTS:], mode="drop")
    received = lax.all_to_all(
        outgoing, ("front", "helper"), split_axis=0, concat_axis=0, tiled=True
    )
    me_flat = my_front * helpers + my_helper
    all_cb = row_list >= PIVOTS
    all_target = jnp.take_along_axis(
        child_map, jnp.clip(row_list - PIVOTS, 0, cb_width - 1), axis=1
    )
    to_me = (all_cb & (all_target // parent_rows == me_flat)).reshape(devices_all, row_count)
    arrive_rank = jnp.cumsum(to_me.astype(jnp.int32), axis=1) - 1
    arrive_slot = jnp.where(to_me, arrive_rank, cap_rows)
    source_iota = jnp.broadcast_to(device_iota[:, None], (devices_all, row_count))
    local_target = (all_target % parent_rows).reshape(devices_all, row_count)
    dest_row = jnp.full((devices_all, cap_rows), parent_rows, jnp.int32)
    dest_row = dest_row.at[source_iota, arrive_slot].set(local_target, mode="drop")
    front_received = received.reshape(fronts, helpers * cap_rows, cb_width)
    front_dest = dest_row.reshape(fronts, helpers * cap_rows)
    front_iota = jnp.arange(fronts, dtype=jnp.int32)
    column_iota = jnp.arange(cb_width, dtype=jnp.int32)
    column_slot = jnp.full((fronts, parent_width), cb_width, jnp.int32)
    column_slot = column_slot.at[front_iota[:, None], child_map].set(
        jnp.broadcast_to(column_iota[None, :], (fronts, cb_width))
    )
    assembled = parent
    for front_index in range(fronts):
        local_block = jnp.zeros((parent_rows, cb_width), jnp.float32)
        local_block = local_block.at[front_dest[front_index]].add(
            front_received[front_index], mode="drop"
        )
        slot_row = column_slot[front_index]
        spread = jnp.take(local_block, jnp.minimum(slot_row, cb_width - 1), axis=1)
        assembled = assembled + jnp.where((slot_row < cb_width)[None, :], spread, 0.0)
    return (front_rows[None], assembled)


def solution(mesh):
    in_specs = (P("front", "helper", None), P(), P(), P(("front", "helper"), None))
    out_specs = (P("front", "helper", None), P(("front", "helper"), None))
    return jax.shard_map(local, mesh=mesh, in_specs=in_specs, out_specs=out_specs, check_vma=False)
```

profile of v0, /device:TPU:9, one launch (start us, length us, event | category | flops | bytes accessed | tf_op | source)
XLA Modules:
  0.0 1328.8 jit_solution(17259688355294850611)
XLA Ops:
  8.3 9.1 gather_fusion
  17.4 5.0 select_select_fusion
  22.5 9.0 copy.35
  36.2 7.9 copy.324
  44.9 59.8 %all-reduce.2.cloned.1.call-done = f32[256,4096]{1,0:T(8,128)} async-done(((f32[256,4096]{1,0:T(8,128)}), f32[256,4096]{1,0:T(8,128)}) %all-reduce.2.cloned.1.call-update) | async-done | bytes 4194320 | tf_op jit(solution)/shard_map/psum | solution.py:64
  669.7 3.5 copy.325
  675.5 11.0 bitcast_dynamic-update-slice_fusion
  686.5 3.4 copy-done.2
  689.9 9.1 copy.46
  699.0 4.0 broadcast_in_dim.168
  703.1 124.7 %scatter_fusion = f32[32,16,3840]{2,1,0:T(8,128)} fusion(f32[32,16,3840]{2,1,0:T(8,128)} %broadcast_in_dim.168, s32[512]{0:T(512)S(1)} %bitcast.894, f32[512,3840]{1,0:T(8,128)} %copy.46), kind=kCustom, calls=%fused_computation.7 | custom fusion | bytes 23597056 | tf_op jit(solution)/shard_map/scatter | solution.py:85
  827.7 5.2 all-to-all-start
  833.5 137.6 %gather_fusion.2 = s32[16384]{0:T(1024)S(1)} fusion(s32[4,3840]{1,0:T(4,128)S(1)} %copy-done, s32[16384]{0:T(1024)S(1)} %bitcast.889), kind=kCustom, calls=%fused_computation.6 | custom fusion | bytes 262144 | tf_op jit(solution)/shard_map/jit(take_along_axis)/gather | solution.py:91
  973.5 60.5 %scatter_custom_fusion.6 = s32[512]{0:T(512)S(1)} fusion(s32[16384]{0:T(1024)S(1)} %bitcast.901, s32[16384]{0:T(1024)S(1)} %bitcast.900, s32[]{:T(128)} %constant.5560.clone.1), kind=kCustom, calls=%fused_computation.748 | custom fusion | bytes 2052
  1034.8 9.0 copy.48
  1043.8 56.6 %scatter_custom_fusion.5 = s32[32768]{0:T(1024)S(1)} fusion(s32[15360]{0:T(1024)S(1)} %reshape.6164, s32[15360]{0:T(1024)S(1)} %reshape.6166, s32[]{:T(128)} %constant.5549.clone.1), kind=kCustom, calls=%fused_computation.125 | custom fusion | bytes 131076
  1100.6 8.9 copy.55
  1109.5 5.9 fusion.138
  1115.5 6.2 scatter_custom_fusion.4
  1121.6 5.5 copy.54
  1127.1 6.4 scatter_custom_fusion.1
  1133.5 5.5 copy.47
  1138.9 6.2 scatter_custom_fusion.3
  1145.1 5.5 copy.52
  1150.5 5.1 scatter_custom_fusion.2
  1155.7 5.5 copy.50
  1161.2 33.4 %gather_fusion.4 = f32[8192,256]{1,0:T(8,128)} fusion(f32[256,3840]{0,1:T(8,128)} %copy.50, s32[8192]{0:T(1024)S(1)} %get-tuple-element.3148), kind=kCustom, calls=%fused_computation.1.clone | custom fusion | bytes 16809984 | tf_op jit(solution)/shard_map/jit(_take)/gather | solution.py:116
  1194.6 33.5 %gather_fusion.5 = f32[8192,256]{1,0:T(8,128)} fusion(f32[256,3840]{0,1:T(8,128)} %copy.52, s32[8192]{0:T(1024)S(1)} %get-tuple-element.3147), kind=kCustom, calls=%fused_computation.2.clone | custom fusion | bytes 16809984 | tf_op jit(solution)/shard_map/jit(_take)/gather | solution.py:116
  1228.1 33.4 %gather_fusion.3 = f32[8192,256]{1,0:T(8,128)} fusion(f32[256,3840]{0,1:T(8,128)} %copy.47, s32[8192]{0:T(1024)S(1)} %get-tuple-element.3146), kind=kCustom, calls=%fused_computation.clone | custom fusion | bytes 16809984 | tf_op jit(solution)/shard_map/jit(_take)/gather | solution.py:116
  1261.5 33.6 %gather_fusion.6 = f32[8192,256]{1,0:T(8,128)} fusion(f32[256,3840]{0,1:T(8,128)} %copy.54, s32[8192]{0:T(1024)S(1)} %get-tuple-element.3149), kind=kCustom, calls=%fused_computation.3.clone | custom fusion | bytes 16809984 | tf_op jit(solution)/shard_map/jit(_take)/gather | solution.py:116
  1295.1 17.4 %fusion = f32[256,8192]{0,1:T(8,128)} fusion(f32[256,8192]{0,1:T(8,128)} %copy.48, f32[8192,256]{1,0:T(8,128)} %gather_fusion.6, f32[8192,256]{1,0:T(8,128)} %gather_fusion.5, f32[8192,256]{1,0:T(8,128)} %gather_fusion.4, f32[8192,256]{1,0:T(8,128)} %gather_fusion.3, pred[8192]{0:T(1024)(128)(4,1)S(1)} %get-tuple-element.3139, ...), kind=kLoop, calls=%fused_computation.15 | loop fusion | flops 25165824 | bytes 50397184 | tf_op jit(solution)/shard_map/add | solution.py:117
  1312.6 8.9 copy.56
  (1665 shorter events, 572.8 us)
Async XLA Ops:
  7.2 97.6 %all-reduce.2.cloned.1.call-start = ((), (), s32[]{:S(2)}) async-start(), calls=%async_computation.1 | async-start | bytes 8388608 | tf_op jit(solution)/shard_map/psum | solution.py:64
  22.5 9.0 copy-start
  669.7 5.8 copy-start.1
  686.5 3.4 copy-start.2
  827.7 5.3 copy-start.7
  827.7 5.4 copy-start.6
  827.7 5.7 copy-start.3
  827.7 281.8 %all-to-all-start = ((f32[32,16,3840]{2,1,0:T(8,128)}), f32[32,16,3840]{2,1,0:T(8,128)}, u32[]{:S(2)}, u32[]{:S(2)}) async-start(f32[32,16,3840]{2,1,0:T(8,128)} %scatter_fusion), calls=%async_computation | async-start | bytes 15728640 | tf_op jit(solution)/shard_map/all_to_all | solution.py:86
  833.5 139.8 %copy-start.5 = (s32[2]{0:T(128)S(1)}, s32[2]{0:T(128)}, u32[]{:S(2)}) copy-start(s32[2]{0:T(128)} %constant.5608) | copy-start | bytes 28
  833.5 139.9 %copy-start.4 = (s32[2]{0:T(128)S(1)}, s32[2]{0:T(128)}, u32[]{:S(2)}) copy-start(s32[2]{0:T(128)} %constant.5611) | copy-start | bytes 28
Sparse Core Ops, SparseCore 0:
  22.6 82.0 all-reduce.1
where the time goes:
time: 1350 us; the launch traced here: 1330 us
  local copies, waits for them, and re-layouts  830 us (61%)
  other arithmetic  386 us (29%)
  waiting for transfers between devices  59.8 us (4%)
  matrix products  28.4 us (2%)
  between operations  19.5 us (1%)
    unnamed x29, local copies, waits for them, and re-layouts  170 us
    div x256, other arithmetic, small_inverse(): pivot_row = augmented[column] / augmented[column, column]  159 us
    mul x248, other arithmetic, small_inverse(): augmented = augmented - augmented[:, column:column + 1] * pivot_row[None, :]  153 us
    slice x256, local copies, waits for them, and re-layouts, small_inverse(): pivot_row = augmented[column] / augmented[column, column]  153 us
    gather x2, local copies, waits for them, and re-layouts, local(): jnp.take_along_axis(child_map, jnp.clip(row_list - PIVOTS, 0, cb_width -...  138 us
    gather x4, local copies, waits for them, and re-layouts, local(): spread = jnp.take(local_block, jnp.minimum(slot_row, cb_width - 1), axis=1)  134 us
    scatter x1, local copies, waits for them, and re-layouts, local(): outgoing.at[owner, dest_rank].set(front_rows[:, PIVOTS:], mode='drop')  125 us
    psum x1, waiting for transfers between devices, local(): panel_rows = lax.psum(picked, 'helper')  59.8 us
  transfers between devices with their start and end apart: 2, of which 1 were waited for; matrix products, arithmetic and copies ran while one was open for 22% of the time, Pallas kernels for 0%

commit v1 on v0

v1 whole, which is shorter than its diff:
```python
import jax
import jax.numpy as jnp
from jax import lax
from jax.experimental import pallas as pl
from jax.experimental.pallas import tpu as pltpu
from jax.sharding import PartitionSpec as P

PANEL = 256
PIVOTS = 256
LANES = 128
BLOCK = 32
CHUNKS = 2


def product(left, right, precision=lax.Precision.HIGHEST):
    return jnp.dot(left, right, precision=precision, preferred_element_type=jnp.float32)


def inverse_kernel(matrix_ref, out_ref):
    extent = matrix_ref.shape[0]
    out_ref[...] = matrix_ref[...]
    row_iota = lax.broadcasted_iota(jnp.int32, (BLOCK, 1), 0)
    lane_iota = lax.broadcasted_iota(jnp.int32, (1, extent), 1)
    for start in range(0, extent, BLOCK):
        rows = out_ref[start : start + BLOCK, :]
        for step in range(BLOCK):
            lane = start + step
            column = rows[:, lane : lane + 1]
            pivot_row = rows[step : step + 1, :]
            scale = 1.0 / column[step : step + 1, :]
            at_lane = lane_iota == lane
            scaled = jnp.where(at_lane, scale, pivot_row * scale)
            weight = jnp.where(row_iota == step, -1.0, column)
            keep = jnp.where(at_lane | (row_iota == step), 0.0, rows)
            rows = keep - weight * scaled
        out_ref[start : start + BLOCK, :] = rows
        tile = start // LANES * LANES
        tile_lane = tile + lax.broadcasted_iota(jnp.int32, (1, LANES), 1)
        all_row = lax.broadcasted_iota(jnp.int32, (extent, 1), 0)
        outside = (all_row < start) | (all_row >= start + BLOCK)
        inside_lane = (tile_lane >= start) & (tile_lane < start + BLOCK)
        left = jnp.where(outside & inside_lane, out_ref[:, tile : tile + LANES], 0.0)
        update = product(left, out_ref[tile : tile + LANES, :])
        cleared = outside & (lane_iota >= start) & (lane_iota < start + BLOCK)
        out_ref[...] = jnp.where(cleared, 0.0, out_ref[...]) - update


def block_inverse(matrix):
    extent = matrix.shape[0]
    return pl.pallas_call(
        inverse_kernel,
        out_shape=jax.ShapeDtypeStruct((extent, extent), jnp.float32),
        in_specs=[pl.BlockSpec(memory_space=pltpu.VMEM)],
        out_specs=pl.BlockSpec(memory_space=pltpu.VMEM),
        compiler_params=pltpu.CompilerParams(vmem_limit_bytes=16 * 1024 * 1024),
        cost_estimate=pl.CostEstimate(flops=10**9, bytes_accessed=10**8, transcendentals=0),
        name="panel_inverse",
    )(matrix)


def spread_kernel(map_ref, target_ref, received_ref, base_ref, out_ref, turned, spread):
    front = pl.program_id(0)
    width = received_ref.shape[2]
    slots = received_ref.shape[1]
    parent_rows, parent_width = out_ref.shape

    @pl.when(front == 0)
    def _():
        out_ref[...] = base_ref[...]

    spread[...] = jnp.zeros_like(spread)
    for first in range(0, width, LANES):
        turned[first : first + LANES, :] = received_ref[0, :, first : first + LANES].T

    @pl.loop(0, width // 16)
    def _(group):
        base = group * 16
        for offset in range(16):
            place = map_ref[front, base + offset]
            spread[pl.ds(place, 1), :] = turned[pl.ds(base + offset, 1), :]

    row_iota = lax.broadcasted_iota(jnp.int32, (parent_rows, slots), 0)
    pick = (row_iota == target_ref[0].astype(jnp.int32)).astype(jnp.bfloat16)
    pick = jnp.concatenate([pick, pick], axis=1)
    piece = 512

    @pl.loop(0, parent_width // piece)
    def _(index):
        at = pl.ds(pl.multiple_of(index * piece, piece), piece)
        block = spread[at, :]
        high = block.astype(jnp.bfloat16)
        low = (block - high.astype(jnp.float32)).astype(jnp.bfloat16)
        both = jnp.concatenate([high, low], axis=1)
        out_ref[:, at] += lax.dot_general(
            pick, both, (((1,), (1,)), ((), ())), preferred_element_type=jnp.float32
        )


def spread_add(columns, targets, received, base):
    fronts, slots, width = received.shape
    parent_rows, parent_width = base.shape
    return pl.pallas_call(
        spread_kernel,
        grid=(fronts,),
        out_shape=jax.ShapeDtypeStruct(base.shape, jnp.float32),
        in_specs=[
            pl.BlockSpec(memory_space=pltpu.SMEM),
            pl.BlockSpec((1, 1, slots), lambda front: (front, 0, 0)),
            pl.BlockSpec((1, slots, width), lambda front: (front, 0, 0)),
            pl.BlockSpec((parent_rows, parent_width), lambda front: (0, 0), pipeline_mode=pl.Buffered(1)),
        ],
        out_specs=pl.BlockSpec((parent_rows, parent_width), lambda front: (0, 0)),
        scratch_shapes=[
            pltpu.VMEM((width, slots), jnp.float32),
            pltpu.VMEM((parent_width, slots), jnp.float32),
        ],
        compiler_params=pltpu.CompilerParams(vmem_limit_bytes=48 * 1024 * 1024),
        cost_estimate=pl.CostEstimate(
            flops=4 * fronts * parent_rows * slots * parent_width,
            bytes_accessed=100 * 10**6,
            transcendentals=0,
        ),
        name="spread_add",
    )(columns, targets, received, base)


def local(front, row_list, child_map, parent):
    front_rows = front[0]
    row_count = front_rows.shape[0]
    helpers = lax.axis_size("helper")
    fronts = lax.axis_size("front")
    devices_all = helpers * fronts
    my_front = lax.axis_index("front")
    my_helper = lax.axis_index("helper")
    parent_rows = parent.shape[0]
    cb_width = front_rows.shape[1] - PIVOTS
    cap_rows = (row_count + devices_all - 1) // devices_all
    cap_panel = 3 * PANEL // (2 * helpers)
    front_order = jnp.take(row_list, my_front, axis=0)
    own_ids = lax.dynamic_slice_in_dim(front_order, my_helper * row_count, row_count)

    by_helper = front_order.reshape(helpers, row_count)
    in_panel = by_helper < PANEL
    panel_rank = jnp.cumsum(in_panel.astype(jnp.int32), axis=1) - 1
    slot_iota = jnp.arange(cap_panel, dtype=jnp.int32)
    in_slot = (panel_rank[:, None, :] == slot_iota[None, :, None]) & in_panel[:, None, :]
    slot_ids = (jnp.sum(jnp.where(in_slot, by_helper[:, None, :] + 1, 0), axis=2) - 1).reshape(-1)
    own_slot = lax.dynamic_index_in_dim(in_slot, my_helper, 0, keepdims=False)
    picked = product(own_slot.astype(jnp.float32), front_rows)
    head = lax.all_gather(picked[:, :PANEL], "helper", axis=0, tiled=True)
    tail = lax.all_gather(picked[:, PANEL:], "helper", axis=0, tiled=True)
    order = (slot_ids[None, :] == jnp.arange(PANEL, dtype=jnp.int32)[:, None]).astype(jnp.float32)

    own_map = jnp.take(child_map, my_front, axis=0)
    own_cb = own_ids >= PIVOTS
    own_target = jnp.take(own_map, jnp.clip(own_ids - PIVOTS, 0, cb_width - 1))
    device_iota = jnp.arange(devices_all, dtype=jnp.int32)
    owner = jnp.where(own_cb, own_target // parent_rows, devices_all)
    dest_match = owner[:, None] == device_iota[None, :]
    dest_rank = jnp.sum(
        jnp.where(dest_match, jnp.cumsum(dest_match.astype(jnp.int32), axis=0) - 1, 0), axis=1
    )
    send_slot = jnp.where(own_cb, owner * cap_rows + dest_rank, -1)
    send_iota = jnp.arange(devices_all * cap_rows, dtype=jnp.int32)
    pack = send_slot[None, :] == send_iota[:, None]
    send_target = jnp.sum(jnp.where(pack, own_target[None, :] % parent_rows + 1, 0), axis=1) - 1
    targets = lax.all_to_all(
        send_target.astype(jnp.float32).reshape(devices_all, cap_rows),
        ("front", "helper"), split_axis=0, concat_axis=0, tiled=True,
    ).reshape(fronts, 1, helpers * cap_rows)
    pack = pack.astype(jnp.float32)

    inverse = block_inverse(product(order, head))
    active = (own_ids >= PANEL)[:, None]
    current = front_rows[:, :PANEL]
    lower_part = jnp.where(active, product(current, inverse), 0.0)
    lower_slots = product(lower_part, order)

    width = cb_width // CHUNKS
    pieces = [jnp.where(active, lower_part, current)]
    assembled = parent
    arrived = []
    for chunk in range(CHUNKS):
        lo = chunk * width
        block = front_rows[:, PANEL + lo : PANEL + lo + width] - product(
            lower_slots, tail[:, lo : lo + width], lax.Precision.HIGH
        )
        pieces.append(block)
        outgoing = product(pack, block, lax.Precision.HIGH)
        arrived.append(lax.all_to_all(
            outgoing.reshape(devices_all, cap_rows, width),
            ("front", "helper"), split_axis=0, concat_axis=0, tiled=True,
        ))
    for chunk in range(CHUNKS):
        lo = chunk * width
        received = arrived[chunk].reshape(fronts, helpers * cap_rows, width)
        assembled = spread_add(child_map[:, lo : lo + width], targets, received, assembled)
    return (jnp.concatenate(pieces, axis=1)[None], assembled)


def solution(mesh):
    in_specs = (P("front", "helper", None), P(), P(), P(("front", "helper"), None))
    out_specs = (P("front", "helper", None), P(("front", "helper"), None))
    return jax.shard_map(local, mesh=mesh, in_specs=in_specs, out_specs=out_specs, check_vma=False)
```

time: 1350 us -> 333 us (0.25); the launches traced: 1330 us -> 329 us
  local copies, waits for them, and re-layouts: 830 us -> 27.6 us
  other arithmetic: 386 us -> 10.8 us
  Pallas kernels: 0 us -> 121 us
  waiting for transfers between devices: 59.8 us -> 95 us
    gather x7 -> x0, local copies, waits for them, and re-layouts: 281 us -> none  [the longest x2 138 us: local(): jnp.take_along_axis(child_map, jnp.clip(row_list - PIVOTS, 0, cb_width -...]
    slice x526 -> x4, local copies, waits for them, and re-layouts: 206 us -> 1.14 us  [the longest x1 0.91 us: local(): tail = lax.all_gather(picked[:, PANEL:], 'helper', axis=0, tiled=True)]
    div x256 -> x0, other arithmetic: 159 us -> none  [small_inverse(): pivot_row = augmented[column] / augmented[column, column]]
    mul x248 -> x0, other arithmetic: 153 us -> none  [small_inverse(): augmented = augmented - augmented[:, column:column + 1] * pivot_row[None, :]]
    unnamed x29 -> x8, local copies, waits for them, and re-layouts: 170 us -> 21.7 us
    scatter x257 -> x0, local copies, waits for them, and re-layouts: 133 us -> none  [the longest x1 125 us: local(): outgoing.at[owner, dest_rank].set(front_rows[:, PIVOTS:], mode='drop')]
    pallas_call x0 -> x3, Pallas kernels: none -> 121 us  [the longest x2 96 us: spread_add(): pl.pallas_call(spread_kernel, grid=(fronts,), out_shape=jax.ShapeDtypeStr...]
    all_to_all x1 -> x3, waiting for transfers between devices: 0.01 us -> 94.9 us  [the longest x2 94.9 us: local(): lax.all_to_all(outgoing.reshape(devices_all, cap_rows, width), ('front',...]
  transfers between devices with their start and end apart: 2 -> 4, of which waited for: 1 -> 2; matrix products, arithmetic and copies ran while one was open for 22% -> 17% of each run, Pallas kernels for 0% -> 22%
where the time goes in v1:
time: 333 us; the launch traced here: 329 us
  Pallas kernels  121 us (36%)
  waiting for transfers between devices  95 us (29%)
  matrix products  31.3 us (9%)
  local copies, waits for them, and re-layouts  27.6 us (8%)
  starting transfers between devices  17.8 us (5%)
  between operations  14.3 us (4%)
  blocking collectives  10.9 us (3%)
  other arithmetic  10.8 us (3%)
    pallas_call x2, Pallas kernels, spread_add(): pl.pallas_call(spread_kernel, grid=(fronts,), out_shape=jax.ShapeDtypeStr...  96 us
    all_to_all x2, waiting for transfers between devices, local(): lax.all_to_all(outgoing.reshape(devices_all, cap_rows, width), ('front',...  94.9 us
    dot_general x8, matrix products, product(): jnp.dot(left, right, precision=precision, preferred_element_type=jnp.floa...  31.3 us
    pallas_call x1, Pallas kernels, block_inverse(): pl.pallas_call(inverse_kernel, out_shape=jax.ShapeDtypeStruct((extent, ex...  25.3 us
    unnamed x8, local copies, waits for them, and re-layouts  21.7 us
    all_to_all x2, starting transfers between devices, local(): lax.all_to_all(outgoing.reshape(devices_all, cap_rows, width), ('front',...  11.4 us
    all_gather x1, blocking collectives, local(): head = lax.all_gather(picked[:, :PANEL], 'helper', axis=0, tiled=True)  10.9 us
  transfers between devices with their start and end apart: 4, of which 2 were waited for; matrix products, arithmetic and copies ran while one was open for 17% of the time, Pallas kernels for 22%

profile of v1, /device:TPU:9, one launch (start us, length us, event | category | flops | bytes accessed | tf_op | source)
XLA Modules:
  0.0 328.9 jit_solution(11899278378317474326)
XLA Ops:
  7.2 0.9 add_reduce_fusion
  8.2 1.1 reduce-window.14
  9.9 6.6 %fusion = f32[48,4096]{1,0:T(8,128)S(1)} fusion(f32[1,512,4096]{2,1,0:T(8,128)} %param.4, pred[8,48,512]{2,1,0:T(8,128)(4,1)S(1)} %fusion.6, s32[]{:T(128)S(6)} %select_n.92), kind=kOutput, calls=%fused_computation.2 | convolution fusion | flops 1207959552 | bytes 9199620 | tf_op jit(solution)/shard_map/dot_general | solution.py:16
  16.5 0.9 slice.72
  17.5 3.1 gather_fusion
  20.8 1.2 reduce-window.16
  21.9 0.2 slice_reduce_fusion
  22.5 0.7 convert_element_type.33
  23.2 6.4 %all-to-all-start = ((f32[32,1,16]{2,1,0:T(1,128)}), f32[32,1,16]{2,1,0:T(1,128)S(1)}, u32[]{:S(2)}, u32[]{:S(2)}) async-start(f32[32,1,16]{2,1,0:T(1,128)} %bitcast.9), calls=%async_computation | async-start | bytes 32768 | tf_op jit(solution)/shard_map/all_to_all | solution.py:167
  29.6 9.0 %copy.29 = f32[1,512,4096]{1,2,0:T(8,128)} copy(f32[1,512,4096]{2,1,0:T(8,128)} %param.4) | data formatting | bytes 16777216 | tf_op args[0]
  38.5 0.3 select_reduce_fusion.1
  38.9 10.9 %all_gather.6 = f32[384,256]{1,0:T(8,128)S(1)} all-gather(f32[48,256]{1,0:T(8,128)S(1)} %slice.69), channel_id=1, replica_groups=mesh['front'=4,'helper'=8] {'helper'}, dimensions={0}, use_global_device_ids=true | all-gather | bytes 442368 | tf_op jit(solution)/shard_map/all_gather | solution.py:150
  49.7 0.4 fusion.11.matrix_ref
  50.2 25.3 %panel_inverse.1 = f32[256,256]{1,0:T(8,128)S(1)} custom-call(f32[256,256]{1,0:T(8,128)S(1)} %fusion.11.matrix_ref), custom_call_target="tpu_custom_call" | custom-call | flops 1000000000 | bytes 100000000 | tf_op jit(solution)/shard_map/panel_inverse/pallas_call | solution.py:50
  75.5 1.8 bitcast_select_fusion
  77.3 0.6 fusion.10
  78.0 6.7 %slice_subtract_fusion.1 = f32[512,1920]{0,1:T(8,128)S(1)} fusion(f32[512,4096]{0,1:T(8,128)} %bitcast.48, f32[512,384]{1,0:T(8,128)S(1)} %fusion.10, f32[384,3840]{1,0:T(8,128)} %all-gather.2.cloned.1.call-done), kind=kOutput, calls=%fused_computation.5 | convolution fusion | flops 2265907200 | bytes 11599872 | tf_op jit(solution)/shard_map/dot_general | solution.py:16
  84.7 1.9 copy-done
  86.7 4.3 %fusion.4 = f32[512,1920]{1,0:T(8,128)} fusion(f32[512,1920]{0,1:T(8,128)S(1)} %slice_subtract_fusion.1, s32[512]{0:T(512)S(1)} %add_select_fusion.2), kind=kOutput, calls=%fused_computation.11 | convolution fusion | flops 3020161024 | bytes 7866368 | tf_op jit(solution)/shard_map/dot_general | solution.py:16
  91.0 4.9 %all-to-all-start.2 = ((f32[32,16,1920]{2,1,0:T(8,128)}), f32[32,16,1920]{2,1,0:T(8,128)}, u32[]{:S(2)}, u32[]{:S(2)}) async-start(f32[32,16,1920]{2,1,0:T(8,128)} %bitcast.51), calls=%async_computation.2 | async-start | bytes 7864320 | tf_op jit(solution)/shard_map/all_to_all | solution.py:190
  95.8 6.5 %slice_subtract_fusion = f32[512,1920]{0,1:T(8,128)S(1)} fusion(f32[512,4096]{0,1:T(8,128)} %bitcast.49, f32[512,384]{1,0:T(8,128)S(1)} %fusion.10, f32[384,3840]{1,0:T(8,128)} %all-gather.2.cloned.1.call-done), kind=kOutput, calls=%fused_computation.4 | convolution fusion | flops 2265907200 | bytes 11599872 | tf_op jit(solution)/shard_map/dot_general | solution.py:16
  102.3 1.9 copy-done.1
  104.3 4.3 %fusion.5 = f32[512,1920]{1,0:T(8,128)} fusion(f32[512,1920]{0,1:T(8,128)S(1)} %slice_subtract_fusion, s32[512]{0:T(512)S(1)} %add_select_fusion.2), kind=kOutput, calls=%fused_computation.12 | convolution fusion | flops 3020161024 | bytes 7866368 | tf_op jit(solution)/shard_map/dot_general | solution.py:16
  108.5 73.1 %all-to-all-done.2 = f32[32,16,1920]{2,1,0:T(8,128)} async-done(((f32[32,16,1920]{2,1,0:T(8,128)}), f32[32,16,1920]{2,1,0:T(8,128)}, u32[]{:S(2)}, u32[]{:S(2)}) %all-to-all-start.2) | async-done | bytes 3932192 | tf_op jit(solution)/shard_map/all_to_all | solution.py:190
  181.6 6.5 %all-to-all-start.1 = ((f32[32,16,1920]{2,1,0:T(8,128)}), f32[32,16,1920]{2,1,0:T(8,128)}, u32[]{:S(2)}, u32[]{:S(2)}) async-start(f32[32,16,1920]{2,1,0:T(8,128)} %bitcast.50), calls=%async_computation.1 | async-start | bytes 7864320 | tf_op jit(solution)/shard_map/all_to_all | solution.py:190
  188.2 0.5 broadcast.231
  188.7 0.7 reduce.17
  189.5 5.8 %maximum_bitcast_fusion = f32[1,512,4096]{1,2,0:T(8,128)} fusion(f32[512,1920]{0,1:T(8,128)} %copy-done.1, f32[512,1920]{0,1:T(8,128)} %copy-done, f32[512,256]{0,1:T(8,128)S(1)} %get-tuple-element.40), kind=kLoop, calls=%fused_computation.1 | loop fusion | flops 4194304 | bytes 16777216 | tf_op jit(solution)/shard_map/broadcast_in_dim | solution.py:198
  195.3 8.9 %copy.36 = f32[1,512,4096]{2,1,0:T(8,128)} copy(f32[1,512,4096]{1,2,0:T(8,128)} %maximum_bitcast_fusion) | data formatting | bytes 16777216
  204.2 47.9 %spread_add.2.base_ref = f32[256,8192]{1,0:T(8,128)} custom-call(s32[4,1920]{1,0:T(4,128)S(1)} %get-tuple-element.34.map_ref, f32[4,1,128]{2,1,0:T(1,128)S(1)} %bitcast.45, f32[4,128,1920]{2,1,0:T(8,128)} %bitcast.15.received_ref, f32[256,8192]{1,0:T(8,128)} %base_ref.1), custom_call_target="tpu_custom_call" | custom-call | flops 4294967296 | bytes 100000000 | tf_op jit(solution)/shard_map/spread_add/pallas_call | solution.py:102
  252.1 21.8 %all-to-all-done.1 = f32[32,16,1920]{2,1,0:T(8,128)} async-done(((f32[32,16,1920]{2,1,0:T(8,128)}), f32[32,16,1920]{2,1,0:T(8,128)}, u32[]{:S(2)}, u32[]{:S(2)}) %all-to-all-start.1) | async-done | bytes 3932192 | tf_op jit(solution)/shard_map/all_to_all | solution.py:190
  273.9 48.1 %spread_add.3 = f32[256,8192]{1,0:T(8,128)} custom-call(s32[4,1920]{1,0:T(4,128)S(1)} %get-tuple-element.35.map_ref, f32[4,1,128]{2,1,0:T(1,128)S(1)} %bitcast.46, f32[4,128,1920]{2,1,0:T(8,128)} %bitcast.12.received_ref, f32[256,8192]{1,0:T(8,128)} %spread_add.2.base_ref), custom_call_target="tpu_custom_call" | custom-call | flops 4294967296 | bytes 100000000 | tf_op jit(solution)/shard_map/spread_add/pallas_call | solution.py:102
  (35 shorter events, 1.3 us)
Async XLA Ops:
  7.2 70.8 %all-gather.2.cloned.1.call-start = ((), (), s32[]{:S(2)}) async-start(), calls=%async_computation.3 | async-start | bytes 6635520 | tf_op jit(solution)/shard_map/all_gather | solution.py:151
  9.9 7.6 %copy-start.2 = (s32[4,3840]{1,0:T(4,128)S(1)}, s32[4,3840]{1,0:T(4,128)}, u32[]{:S(2)}) copy-start(s32[4,3840]{1,0:T(4,128)} %param.6) | copy-start | bytes 184324
  23.2 67.8 %all-to-all-start = ((f32[32,1,16]{2,1,0:T(1,128)}), f32[32,1,16]{2,1,0:T(1,128)S(1)}, u32[]{:S(2)}, u32[]{:S(2)}) async-start(f32[32,1,16]{2,1,0:T(1,128)} %bitcast.9), calls=%async_computation | async-start | bytes 32768 | tf_op jit(solution)/shard_map/all_to_all | solution.py:167
  84.7 1.9 copy-start
  91.0 90.7 %all-to-all-start.2 = ((f32[32,16,1920]{2,1,0:T(8,128)}), f32[32,16,1920]{2,1,0:T(8,128)}, u32[]{:S(2)}, u32[]{:S(2)}) async-start(f32[32,16,1920]{2,1,0:T(8,128)} %bitcast.51), calls=%async_computation.2 | async-start | bytes 7864320 | tf_op jit(solution)/shard_map/all_to_all | solution.py:190
  102.3 1.9 copy-start.1
  181.6 92.3 %all-to-all-start.1 = ((f32[32,16,1920]{2,1,0:T(8,128)}), f32[32,16,1920]{2,1,0:T(8,128)}, u32[]{:S(2)}, u32[]{:S(2)}) async-start(f32[32,16,1920]{2,1,0:T(8,128)} %bitcast.50), calls=%async_computation.1 | async-start | bytes 7864320 | tf_op jit(solution)/shard_map/all_to_all | solution.py:190
Sparse Core Ops, SparseCore 0:
  17.5 46.6 all-gather.1

commit v2 on v1

v2 whole, which is shorter than its diff:
```python
import jax
import jax.numpy as jnp
from jax import lax
from jax.experimental import pallas as pl
from jax.experimental.pallas import tpu as pltpu
from jax.sharding import PartitionSpec as P

PANEL = 256
PIVOTS = 256
LANES = 128
BLOCK = 32
TILE = 256
WINDOW = 6


def product(left, right, precision=lax.Precision.HIGHEST):
    return jnp.dot(left, right, precision=precision, preferred_element_type=jnp.float32)


def inverse_kernel(matrix_ref, out_ref):
    extent = matrix_ref.shape[0]
    out_ref[...] = matrix_ref[...]
    row_iota = lax.broadcasted_iota(jnp.int32, (BLOCK, 1), 0)
    lane_iota = lax.broadcasted_iota(jnp.int32, (1, extent), 1)
    for start in range(0, extent, BLOCK):
        rows = out_ref[start : start + BLOCK, :]
        for step in range(BLOCK):
            lane = start + step
            column = rows[:, lane : lane + 1]
            pivot_row = rows[step : step + 1, :]
            scale = 1.0 / column[step : step + 1, :]
            at_lane = lane_iota == lane
            scaled = jnp.where(at_lane, scale, pivot_row * scale)
            weight = jnp.where(row_iota == step, -1.0, column)
            keep = jnp.where(at_lane | (row_iota == step), 0.0, rows)
            rows = keep - weight * scaled
        out_ref[start : start + BLOCK, :] = rows
        tile = start // LANES * LANES
        tile_lane = tile + lax.broadcasted_iota(jnp.int32, (1, LANES), 1)
        all_row = lax.broadcasted_iota(jnp.int32, (extent, 1), 0)
        outside = (all_row < start) | (all_row >= start + BLOCK)
        inside_lane = (tile_lane >= start) & (tile_lane < start + BLOCK)
        left = jnp.where(outside & inside_lane, out_ref[:, tile : tile + LANES], 0.0)
        update = product(left, out_ref[tile : tile + LANES, :])
        cleared = outside & (lane_iota >= start) & (lane_iota < start + BLOCK)
        out_ref[...] = jnp.where(cleared, 0.0, out_ref[...]) - update


def block_inverse(matrix):
    extent = matrix.shape[0]
    return pl.pallas_call(
        inverse_kernel,
        out_shape=jax.ShapeDtypeStruct((extent, extent), jnp.float32),
        in_specs=[pl.BlockSpec(memory_space=pltpu.VMEM)],
        out_specs=pl.BlockSpec(memory_space=pltpu.VMEM),
        compiler_params=pltpu.CompilerParams(vmem_limit_bytes=16 * 1024 * 1024),
        cost_estimate=pl.CostEstimate(flops=10**9, bytes_accessed=10**8, transcendentals=0),
        name="panel_inverse",
    )(matrix)


def split(value):
    high = value.astype(jnp.bfloat16)
    return high, (value - high.astype(jnp.float32)).astype(jnp.bfloat16)


def dot(left, right):
    return jnp.dot(left, right, preferred_element_type=jnp.float32)


def outer_update(low_high, low_low, tail):
    tail_high, tail_low = split(tail)
    return dot(low_high, tail_high) + dot(low_high, tail_low) + dot(low_low, tail_high)


def send_kernel(pick_ref, lower_ref, front_ref, tail_ref, *refs):
    out_refs, high_ref, low_ref = refs[:-2], refs[-2], refs[-1]

    @pl.when(pl.program_id(0) == 0)
    def _():
        high_ref[...], low_ref[...] = split(lower_ref[...])

    front_high, front_low = split(front_ref[...])
    pick = pick_ref[...]
    block = dot(pick, front_high) + dot(pick, front_low)
    block = block - outer_update(high_ref[...], low_ref[...], tail_ref[...])
    rows = out_refs[0].shape[0]
    for index, out_ref in enumerate(out_refs):
        out_ref[...] = block[index * rows : (index + 1) * rows]


def send_rows(pick, lower, front_rows, tail, devices_all):
    slots, row_count = pick.shape
    panel_slots, width = tail.shape
    rows = slots // devices_all
    skip = (front_rows.shape[1] - width) // TILE
    fixed = lambda shape: pl.BlockSpec(shape, lambda tile: (0, 0))
    return pl.pallas_call(
        send_kernel,
        grid=(width // TILE,),
        out_shape=[jax.ShapeDtypeStruct((rows, width), jnp.float32)] * devices_all,
        in_specs=[
            fixed(pick.shape),
            fixed(lower.shape),
            pl.BlockSpec((row_count, TILE), lambda tile: (0, tile + skip)),
            pl.BlockSpec((panel_slots, TILE), lambda tile: (0, tile)),
        ],
        out_specs=[pl.BlockSpec((rows, TILE), lambda tile: (0, tile))] * devices_all,
        scratch_shapes=[pltpu.VMEM(lower.shape, jnp.bfloat16)] * 2,
        compiler_params=pltpu.CompilerParams(vmem_limit_bytes=60 * 1024 * 1024),
        cost_estimate=pl.CostEstimate(flops=10**10, bytes_accessed=3 * 10**7, transcendentals=0),
        name="send_rows",
    )(pick, lower, front_rows, tail)


def factor_kernel(left_ref, lower_ref, front_ref, tail_ref, out_ref, high_ref, low_ref):
    tile = pl.program_id(0)

    @pl.when(tile == 0)
    def _():
        out_ref[...] = left_ref[...]
        high_ref[...], low_ref[...] = split(lower_ref[...])

    @pl.when(tile > 0)
    def _():
        out_ref[...] = front_ref[...] - outer_update(high_ref[...], low_ref[...], tail_ref[...])


def factor_rows(left, lower, front_rows, tail):
    row_count, order = front_rows.shape
    panel_slots = tail.shape[0]
    fixed = lambda shape: pl.BlockSpec(shape, lambda tile: (0, 0))
    return pl.pallas_call(
        factor_kernel,
        grid=(order // TILE,),
        out_shape=jax.ShapeDtypeStruct(front_rows.shape, jnp.float32),
        in_specs=[
            fixed(left.shape),
            fixed(lower.shape),
            pl.BlockSpec((row_count, TILE), lambda tile: (0, tile)),
            pl.BlockSpec((panel_slots, TILE), lambda tile: (0, jnp.maximum(tile - 1, 0))),
        ],
        out_specs=pl.BlockSpec((row_count, TILE), lambda tile: (0, tile)),
        scratch_shapes=[pltpu.VMEM(lower.shape, jnp.bfloat16)] * 2,
        compiler_params=pltpu.CompilerParams(vmem_limit_bytes=60 * 1024 * 1024),
        cost_estimate=pl.CostEstimate(flops=10**10, bytes_accessed=3 * 10**7, transcendentals=0),
        name="factor_rows",
    )(left, lower, front_rows, tail)


def spread_kernel(map_ref, target_ref, base_ref, *refs):
    received_refs, out_ref, turned, spread = refs[:-3], refs[-3], refs[-2], refs[-1]
    index = pl.program_id(0)
    width, slots = turned.shape
    parent_rows, piece = out_ref.shape

    @pl.when(index == 0)
    def _():
        spread[...] = jnp.zeros_like(spread)
        for first in range(0, width, LANES):
            parts = [ref[:, first : first + LANES] for ref in received_refs]
            block = jnp.concatenate(parts, axis=0) if len(parts) > 1 else parts[0]
            turned[first : first + LANES, :] = block.T

        @pl.loop(0, width // 16)
        def _(group):
            base = group * 16
            for offset in range(16):
                place = map_ref[base + offset]
                spread[pl.ds(place, 1), :] = turned[pl.ds(base + offset, 1), :]

    row_iota = lax.broadcasted_iota(jnp.int32, (parent_rows, slots), 0)
    pick = (row_iota == target_ref[...].astype(jnp.int32)).astype(jnp.bfloat16)
    pick = jnp.concatenate([pick, pick], axis=1)
    at = pl.ds(pl.multiple_of(index * piece, piece), piece)
    both = jnp.concatenate(split(spread[at, :]), axis=1)
    out_ref[...] = base_ref[...] + lax.dot_general(
        pick, both, (((1,), (1,)), ((), ())), preferred_element_type=jnp.float32
    )


def spread_add(columns, targets, received, base):
    width = columns.shape[0]
    slots = targets.shape[1]
    parent_rows, parent_width = base.shape
    piece = 1024
    block = pl.BlockSpec((parent_rows, piece), lambda index: (0, index))
    whole = lambda array: pl.BlockSpec(array.shape, lambda index: (0, 0))
    return pl.pallas_call(
        spread_kernel,
        grid=(parent_width // piece,),
        out_shape=jax.ShapeDtypeStruct(base.shape, jnp.float32),
        in_specs=[pl.BlockSpec(memory_space=pltpu.SMEM), whole(targets), block]
        + [whole(array) for array in received],
        out_specs=block,
        scratch_shapes=[
            pltpu.VMEM((width, slots), jnp.float32),
            pltpu.VMEM((parent_width, slots), jnp.float32),
        ],
        compiler_params=pltpu.CompilerParams(vmem_limit_bytes=60 * 1024 * 1024),
        cost_estimate=pl.CostEstimate(flops=10**10, bytes_accessed=5 * 10**7, transcendentals=0),
        name="spread_add",
    )(columns, targets, base, *received)


def local(front, row_list, child_map, parent):
    front_rows = front[0]
    row_count = front_rows.shape[0]
    helpers = lax.axis_size("helper")
    fronts = lax.axis_size("front")
    devices_all = helpers * fronts
    my_front = lax.axis_index("front")
    my_helper = lax.axis_index("helper")
    parent_rows = parent.shape[0]
    cb_width = front_rows.shape[1] - PIVOTS
    cap_rows = (row_count + devices_all - 1) // devices_all
    cap_panel = 3 * PANEL // (2 * helpers)
    front_order = jnp.take(row_list, my_front, axis=0)
    own_ids = lax.dynamic_slice_in_dim(front_order, my_helper * row_count, row_count)

    by_helper = front_order.reshape(helpers, row_count)
    in_panel = by_helper < PANEL
    panel_rank = jnp.cumsum(in_panel.astype(jnp.int32), axis=1) - 1
    slot_iota = jnp.arange(cap_panel, dtype=jnp.int32)
    in_slot = (panel_rank[:, None, :] == slot_iota[None, :, None]) & in_panel[:, None, :]
    slot_ids = (jnp.sum(jnp.where(in_slot, by_helper[:, None, :] + 1, 0), axis=2) - 1).reshape(-1)
    own_slot = lax.dynamic_index_in_dim(in_slot, my_helper, 0, keepdims=False)
    own_slot = own_slot.astype(jnp.float32)
    head = lax.all_gather(product(own_slot, front_rows[:, :PANEL]), "helper", axis=0, tiled=True)
    tail = lax.all_gather(product(own_slot, front_rows[:, PANEL:]), "helper", axis=0, tiled=True)
    order = (slot_ids[None, :] == jnp.arange(PANEL, dtype=jnp.int32)[:, None]).astype(jnp.float32)

    own_map = jnp.take(child_map, my_front, axis=0)
    own_cb = own_ids >= PIVOTS
    own_target = jnp.take(own_map, jnp.clip(own_ids - PIVOTS, 0, cb_width - 1))
    device_iota = jnp.arange(devices_all, dtype=jnp.int32)
    owner = jnp.where(own_cb, own_target // parent_rows, devices_all)
    dest_match = owner[:, None] == device_iota[None, :]
    dest_rank = jnp.sum(
        jnp.where(dest_match, jnp.cumsum(dest_match.astype(jnp.int32), axis=0) - 1, 0), axis=1
    )
    me_flat = my_front * helpers + my_helper
    send_slot = jnp.where(own_cb, (owner ^ me_flat) * cap_rows + dest_rank, -1)
    send_iota = jnp.arange(devices_all * cap_rows, dtype=jnp.int32)
    pack = send_slot[None, :] == send_iota[:, None]
    send_target = jnp.sum(jnp.where(pack, own_target[None, :] % parent_rows + 1, 0), axis=1) - 1
    targets = lax.all_to_all(
        jnp.take(send_target.astype(jnp.float32).reshape(devices_all, cap_rows), device_iota ^ me_flat, axis=0),
        ("front", "helper"), split_axis=0, concat_axis=0, tiled=True,
    )
    targets = jnp.take(targets, device_iota ^ me_flat, axis=0).reshape(fronts, 1, helpers * cap_rows)

    inverse = block_inverse(product(order, head))
    active = (own_ids >= PANEL)[:, None]
    current = front_rows[:, :PANEL]
    lower_part = jnp.where(active, product(current, inverse), 0.0)
    lower_slots = product(lower_part, order)

    pack_lower = product(pack.astype(jnp.float32), lower_slots)
    outgoing = send_rows(pack.astype(jnp.bfloat16), pack_lower, front_rows, tail, devices_all)
    near = [offset for offset in range(1, devices_all // 2)]
    far = [offset for offset in range(devices_all // 2, devices_all)]
    sequence = []
    while near or far:
        sequence += far[:1] + near[:2]
        far, near = far[1:], near[2:]
    arrived = list(outgoing)
    for index, offset in enumerate(sequence):
        pairs = [(device, device ^ offset) for device in range(devices_all)]
        piece = outgoing[offset]
        if index >= WINDOW:
            before = sequence[index - WINDOW]
            piece, arrived[before] = lax.optimization_barrier((piece, arrived[before]))
        arrived[offset] = lax.ppermute(piece, ("front", "helper"), pairs)
    factors = factor_rows(jnp.where(active, lower_part, current), lower_slots, front_rows, tail)
    assembled = parent
    for front_offset in range(fronts):
        columns = jnp.take(child_map, my_front ^ front_offset, axis=0)
        received = arrived[front_offset * helpers : (front_offset + 1) * helpers]
        if cap_rows % 8:
            received = [jnp.concatenate(received, axis=0)]
        assembled = spread_add(columns, targets[front_offset], received, assembled)
    return (factors[None], assembled)


def solution(mesh):
    in_specs = (P("front", "helper", None), P(), P(), P(("front", "helper"), None))
    out_specs = (P("front", "helper", None), P(("front", "helper"), None))
    return jax.shard_map(local, mesh=mesh, in_specs=in_specs, out_specs=out_specs, check_vma=False)
```

time: 333 us -> 318 us (0.955)
  starting transfers between devices: 17.8 us -> 47.6 us
  waiting for transfers between devices: 95 us -> 70.7 us
  blocking collectives: 10.9 us -> 31.4 us
  local copies, waits for them, and re-layouts: 27.6 us -> 8.28 us
  matrix products: 31.3 us -> 14.1 us
  other arithmetic: 10.8 us -> 6.08 us
    all_to_all x3 -> x0, waiting for transfers between devices: 94.9 us -> none  [the longest x2 94.9 us: local(): lax.all_to_all(outgoing.reshape(devices_all, cap_rows, width), ('front',...]
    ppermute x0 -> x31, waiting for transfers between devices: none -> 70.6 us  [local(): arrived[offset] = lax.ppermute(piece, ('front', 'helper'), pairs)]
    ppermute x0 -> x31, starting transfers between devices: none -> 47.5 us  [local(): arrived[offset] = lax.ppermute(piece, ('front', 'helper'), pairs)]
    unnamed x8 -> x82, local copies, waits for them, and re-layouts: 21.7 us -> 0.85 us
    all_to_all x0 -> x1, blocking collectives: none -> 19.7 us  [local(): lax.all_to_all(jnp.take(send_target.astype(jnp.float32).reshape(devices_a...]
    all_to_all x3 -> x0, starting transfers between devices: 17.8 us -> none  [the longest x2 11.4 us: local(): lax.all_to_all(outgoing.reshape(devices_all, cap_rows, width), ('front',...]
    dot_general x8 -> x6, matrix products: 31.3 us -> 14.1 us  [product(): jnp.dot(left, right, precision=precision, preferred_element_type=jnp.floa...]
    broadcast_in_dim x1 -> x0, other arithmetic: 5.84 us -> none  [local(): return (jnp.concatenate(pieces, axis=1)[None], assembled)]
  transfers between devices with their start and end apart: 4 -> 32, of which waited for: 2 -> 8; matrix products, arithmetic and copies ran while one was open for 17% -> 6% of each run, Pallas kernels for 22% -> 28%
where the time goes in v2:
time: 318 us; the launch traced here: 316 us
  Pallas kernels  123 us (39%)
  waiting for transfers between devices  70.7 us (22%)
  starting transfers between devices  47.6 us (15%)
  blocking collectives  31.4 us (10%)
  between operations  14.6 us (5%)
  matrix products  14.1 us (4%)
  local copies, waits for them, and re-layouts  8.28 us (3%)
  other arithmetic  6.08 us (2%)
    ppermute x31, waiting for transfers between devices, local(): arrived[offset] = lax.ppermute(piece, ('front', 'helper'), pairs)  70.6 us
    pallas_call x4, Pallas kernels, spread_add(): pl.pallas_call(spread_kernel, grid=(parent_width // piece,), out_shape=ja...  61.9 us
    ppermute x31, starting transfers between devices, local(): arrived[offset] = lax.ppermute(piece, ('front', 'helper'), pairs)  47.5 us
    pallas_call x1, Pallas kernels, block_inverse(): pl.pallas_call(inverse_kernel, out_shape=jax.ShapeDtypeStruct((extent, ex...  25.3 us
    all_to_all x1, blocking collectives, local(): lax.all_to_all(jnp.take(send_target.astype(jnp.float32).reshape(devices_a...  19.7 us
    pallas_call x1, Pallas kernels, send_rows(): pl.pallas_call(send_kernel, grid=(width // TILE,), out_shape=[jax.ShapeDt...  18.7 us
    pallas_call x1, Pallas kernels, factor_rows(): pl.pallas_call(factor_kernel, grid=(order // TILE,), out_shape=jax.ShapeD...  17.3 us
    dot_general x6, matrix products, product(): jnp.dot(left, right, precision=precision, preferred_element_type=jnp.floa...  14.1 us
  transfers between devices with their start and end apart: 32, of which 8 were waited for; matrix products, arithmetic and copies ran while one was open for 6% of the time, Pallas kernels for 28%

profile of v2, /device:TPU:9, one launch (start us, length us, event | category | flops | bytes accessed | tf_op | source)
XLA Modules:
  0.0 315.9 jit_solution(1691126410972973128)
XLA Ops:
  9.9 7.2 %fusion = f32[48,3840]{1,0:T(8,128)} fusion(f32[512,4096]{1,0:T(8,128)} %bitcast.37, pred[8,48,512]{2,1,0:T(8,128)(4,1)S(1)} %fusion.4, s32[]{:T(128)S(6)} %select_n.99), kind=kOutput, calls=%fused_computation.3 | convolution fusion | flops 1132462080 | bytes 8626180 | tf_op jit(solution)/shard_map/dot_general | solution.py:17
  18.3 3.1 gather_fusion
  24.3 11.8 %all_gather.6 = f32[384,256]{1,0:T(8,128)S(1)} all-gather(f32[48,256]{1,0:T(8,128)S(1)} %fusion.7), channel_id=1, replica_groups=mesh['front'=4,'helper'=8] {'helper'}, dimensions={0}, use_global_device_ids=true | all-gather | bytes 442368 | tf_op jit(solution)/shard_map/all_gather | solution.py:229
  36.5 25.3 %panel_inverse.1 = f32[256,256]{1,0:T(8,128)S(1)} custom-call(f32[256,256]{1,0:T(8,128)S(1)} %fusion.10.matrix_ref), custom_call_target="tpu_custom_call" | custom-call | flops 1000000000 | bytes 100000000 | tf_op jit(solution)/shard_map/panel_inverse/pallas_call | solution.py:51
  63.0 2.6 bitcast_select_fusion
  66.3 1.9 fusion.2.lower_ref
  68.2 18.7 %send_rows.1 = (f32[16,3840]{1,0:T(8,128)}, f32[16,3840]{1,0:T(8,128)}, f32[16,3840]{1,0:T(8,128)}, f32[16,3840]{1,0:T(8,128)}, f32[16,3840]{1,0:T(8,128)}, /*in...) custom-call(bf16[512,512]{1,0:T(8,128)(2,1)} %fusion.3.pick_ref, ...), custom_call_target="tpu_custom_call" | custom-call | flops 10000000000 | bytes 30000000 | tf_op jit(solution)/shard_map/send_rows/pallas_call | solution.py:98
  86.9 2.4 collective-permute-start.15
  91.9 13.8 %collective-permute-done.15.refs_0_ = f32[16,3840]{1,0:T(8,128)S(1)} collective-permute-done((f32[16,3840]{1,0:T(8,128)}, f32[16,3840]{1,0:T(8,128)S(1)}, u32[]{:S(2)}, u32[]{:S(2)}) %collective-permute-start.15) | collective-permute-done | bytes 245792 | tf_op jit(solution)/shard_map/ppermute | solution.py:274
  106.9 4.1 %collective-permute-done.16.refs_1_ = f32[16,3840]{1,0:T(8,128)S(1)} collective-permute-done((f32[16,3840]{1,0:T(8,128)}, f32[16,3840]{1,0:T(8,128)S(1)}, u32[]{:S(2)}, u32[]{:S(2)}) %collective-permute-start.16) | collective-permute-done | bytes 245792 | tf_op jit(solution)/shard_map/ppermute | solution.py:274
  111.0 3.9 %collective-permute-start.17 = (f32[16,3840]{1,0:T(8,128)}, f32[16,3840]{1,0:T(8,128)S(1)}, u32[]{:S(2)}, u32[]{:S(2)}) collective-permute-start(f32[16,3840]{1,0:T(8,128)} %get-tuple-element.139), channel_id=1, source_target_pairs={{0,18},{1,19},{2,16},{3,17},{4,22},{5,23},{6,20},{7,21},{8,26},{9,... | collective-permute-start | bytes 737288 | tf_op jit(solution)/shard_map/ppermute | solution.py:274
  117.5 19.7 %all_to_all.12 = f32[32,1,16]{2,1,0:T(1,128)S(1)} all-to-all(f32[32,1,16]{2,1,0:T(1,128)S(1)} %bitcast.44), channel_id=1, replica_groups=mesh['front'=4,'helper'=8] {'front','helper'}, dimensions={0} | all-to-all | bytes 4096 | tf_op jit(solution)/shard_map/all_to_all | solution.py:247
  141.4 3.6 %collective-permute-start.20 = (f32[16,3840]{1,0:T(8,128)}, f32[16,3840]{1,0:T(8,128)S(1)}, u32[]{:S(2)}, u32[]{:S(2)}) collective-permute-start(f32[16,3840]{1,0:T(8,128)} %get-tuple-element.148), channel_id=1, source_target_pairs={{0,21},{1,20},{2,23},{3,22},{4,17},{5,16},{6,19},{7,18},{8,29},{9,... | collective-permute-start | bytes 737288 | tf_op jit(solution)/shard_map/ppermute | solution.py:274
  147.6 2.3 collective-permute-start.10
  149.9 12.9 %collective-permute-done.4.refs_5_ = f32[16,3840]{1,0:T(8,128)S(1)} collective-permute-done((f32[16,3840]{1,0:T(8,128)}, f32[16,3840]{1,0:T(8,128)S(1)}, u32[]{:S(2)}, u32[]{:S(2)}) %collective-permute-start.4) | collective-permute-done | bytes 245792 | tf_op jit(solution)/shard_map/ppermute | solution.py:274
  162.8 2.0 collective-permute-start.8
  165.3 3.7 %collective-permute-start.21 = (f32[16,3840]{1,0:T(8,128)}, f32[16,3840]{1,0:T(8,128)}, u32[]{:S(2)}, u32[]{:S(2)}) collective-permute-start(f32[16,3840]{1,0:T(8,128)} %get-tuple-element.151), channel_id=1, source_target_pairs={{0,22},{1,23},{2,20},{3,21},{4,18},{5,19},{6,16},{7,17},{8,30},{9,... | collective-permute-start | bytes 737288 | tf_op jit(solution)/shard_map/ppermute | solution.py:274
  169.0 17.3 %factor_rows.1 = f32[512,4096]{1,0:T(8,128)} custom-call(f32[512,256]{1,0:T(8,128)} %get-tuple-element.204.left_ref, f32[512,384]{1,0:T(8,128)} %copy-done.1, f32[512,4096]{1,0:T(8,128)} %bitcast.41, f32[384,3840]{1,0:T(8,128)} %all-gather.2.cloned.1.call-done.tail_ref), custom_call_target="tpu_custom_call" | custom-call | flops 10000000000 | bytes 30000000 | tf_op jit(solution)/shard_map/factor_rows/pallas_call | solution.py:133
  186.4 1.6 collective-permute-start.22
  188.0 2.5 collective-permute-start.14
  190.7 3.9 %collective-permute-start.12 = (f32[16,3840]{1,0:T(8,128)S(1)}, f32[16,3840]{1,0:T(8,128)S(1)}, u32[]{:S(2)}, u32[]{:S(2)}) collective-permute-start(f32[16,3840]{1,0:T(8,128)S(1)} %copy-done.14), channel_id=1, source_target_pairs={{0,13},{1,12},{2,15},{3,14},{4,9},{5,8},{6,11},{7,10},{8,5},{9,4},... | collective-permute-start | bytes 737288 | tf_op jit(solution)/shard_map/ppermute | solution.py:274
  194.7 15.5 %spread_add.4.base_ref = f32[256,8192]{1,0:T(8,128)} custom-call(s32[3840]{0:T(1024)} %copy-done, f32[1,128]{1,0:T(1,128)} %squeeze.24.target_ref, f32[256,8192]{1,0:T(8,128)} %base_ref.1, f32[16,3840]{1,0:T(8,128)} %get-tuple-element.86.refs_0_, f32[16,3840]{1,0:T(8,128)} %copy-done.22, f32[16,3840]{1,0:T(8,128)} %copy-done.20, f32[16,3840]{1,0:T(8,128)} %copy-done.19, ...), custom_call_target="tpu_custom_call" | custom-call | flops 10000000000 | bytes 50000000 | tf_op jit(solution)/shard_map/spread_add/pallas_call | solution.py:189
  211.5 2.0 collective-permute-done.12.refs_5_
  213.5 1.8 collective-permute-start.29
  216.4 1.9 collective-permute-start.28
  219.1 15.5 %spread_add.5.base_ref = f32[256,8192]{1,0:T(8,128)} custom-call(s32[3840]{0:T(1024)} %get-tuple-element.190.map_ref, f32[1,128]{1,0:T(1,128)} %squeeze.23.target_ref, f32[256,8192]{1,0:T(8,128)} %spread_add.4.base_ref, f32[16,3840]{1,0:T(8,128)} %copy-done.25, f32[16,3840]{1,0:T(8,128)} %collective-permute-done.8.refs_1_, ...), custom_call_target="tpu_custom_call" | custom-call | flops 10000000000 | bytes 50000000 | tf_op jit(solution)/shard_map/spread_add/pallas_call | solution.py:189
  234.6 26.0 %collective-permute-done.24.refs_1_ = f32[16,3840]{1,0:T(8,128)S(1)} collective-permute-done((f32[16,3840]{1,0:T(8,128)S(1)}, f32[16,3840]{1,0:T(8,128)S(1)}, u32[]{:S(2)}, u32[]{:S(2)}) %collective-permute-start.24) | collective-permute-done | bytes 245792 | tf_op jit(solution)/shard_map/ppermute | solution.py:274
  261.8 4.3 %collective-permute-done.29.refs_6_ = f32[16,3840]{1,0:T(8,128)S(1)} collective-permute-done((f32[16,3840]{1,0:T(8,128)S(1)}, f32[16,3840]{1,0:T(8,128)S(1)}, u32[]{:S(2)}, u32[]{:S(2)}) %collective-permute-start.29) | collective-permute-done | bytes 245792 | tf_op jit(solution)/shard_map/ppermute | solution.py:274
  266.1 3.8 %collective-permute-start.30 = (f32[16,3840]{1,0:T(8,128)S(1)}, f32[16,3840]{1,0:T(8,128)S(1)}, u32[]{:S(2)}, u32[]{:S(2)}) collective-permute-start(f32[16,3840]{1,0:T(8,128)S(1)} %copy-done.3), channel_id=1, source_target_pairs={{0,31},{1,30},{2,29},{3,28},{4,27},{5,26},{6,25},{7,24},{8,23},{9,... | collective-permute-start | bytes 737288 | tf_op jit(solution)/shard_map/ppermute | solution.py:274
  270.0 15.4 %spread_add.6.base_ref = f32[256,8192]{1,0:T(8,128)} custom-call(s32[3840]{0:T(1024)} %get-tuple-element.193.map_ref, f32[1,128]{1,0:T(1,128)} %squeeze.22.target_ref, f32[256,8192]{1,0:T(8,128)} %spread_add.5.base_ref, f32[16,3840]{1,0:T(8,128)} %copy-done.9, f32[16,3840]{1,0:T(8,128)} %copy-done.10, f32[16,3840]{1,0:T(8,128)} %copy-done.12, ...), custom_call_target="tpu_custom_call" | custom-call | flops 10000000000 | bytes 50000000 | tf_op jit(solution)/shard_map/spread_add/pallas_call | solution.py:189
  287.0 6.0 %collective-permute-done.30.refs_7_ = f32[16,3840]{1,0:T(8,128)S(1)} collective-permute-done((f32[16,3840]{1,0:T(8,128)S(1)}, f32[16,3840]{1,0:T(8,128)S(1)}, u32[]{:S(2)}, u32[]{:S(2)}) %collective-permute-start.30) | collective-permute-done | bytes 245792 | tf_op jit(solution)/shard_map/ppermute | solution.py:274
  293.7 15.4 %spread_add.7 = f32[256,8192]{1,0:T(8,128)} custom-call(s32[3840]{0:T(1024)} %get-tuple-element.192.map_ref, f32[1,128]{1,0:T(1,128)} %squeeze.21.target_ref, f32[256,8192]{1,0:T(8,128)} %spread_add.6.base_ref, f32[16,3840]{1,0:T(8,128)} %copy-done.30, f32[16,3840]{1,0:T(8,128)} %copy-done.31, f32[16,3840]{1,0:T(8,128)} %copy-done.39, ...), custom_call_target="tpu_custom_call" | custom-call | flops 10000000000 | bytes 50000000 | tf_op jit(solution)/shard_map/spread_add/pallas_call | solution.py:189
  (174 shorter events, 29.3 us)
Async XLA Ops:
  7.2 61.0 %all-gather.2.cloned.1.call-start = ((), (), s32[]{:S(2)}) async-start(), calls=%async_computation.1 | async-start | bytes 6635520 | tf_op jit(solution)/shard_map/all_gather | solution.py:230
  86.9 18.8 %collective-permute-start.15 = (f32[16,3840]{1,0:T(8,128)}, f32[16,3840]{1,0:T(8,128)S(1)}, u32[]{:S(2)}, u32[]{:S(2)}) collective-permute-start(f32[16,3840]{1,0:T(8,128)} %get-tuple-element.133), channel_id=1, source_target_pairs={{0,16},{1,17},{2,18},{3,19},{4,20},{5,21},{6,22},{7,23},{8,24},{9,... | collective-permute-start | bytes 737288 | tf_op jit(solution)/shard_map/ppermute | solution.py:274
  89.3 21.7 %collective-permute-start.16 = (f32[16,3840]{1,0:T(8,128)}, f32[16,3840]{1,0:T(8,128)S(1)}, u32[]{:S(2)}, u32[]{:S(2)}) collective-permute-start(f32[16,3840]{1,0:T(8,128)} %get-tuple-element.136), channel_id=1, source_target_pairs={{0,17},{1,16},{2,19},{3,18},{4,21},{5,20},{6,23},{7,22},{8,25},{9,... | collective-permute-start | bytes 737288 | tf_op jit(solution)/shard_map/ppermute | solution.py:274
  89.7 25.2 %collective-permute-start.2 = (f32[16,3840]{1,0:T(8,128)}, f32[16,3840]{1,0:T(8,128)S(1)}, u32[]{:S(2)}, u32[]{:S(2)}) collective-permute-start(f32[16,3840]{1,0:T(8,128)} %get-tuple-element.94), channel_id=1, source_target_pairs={{0,3},{1,2},{2,1},{3,0},{4,7},{5,6},{6,5},{7,4},{8,11},{9,10},{10,... | collective-permute-start | bytes 737288 | tf_op jit(solution)/shard_map/ppermute | solution.py:274
  90.9 24.4 %collective-permute-start.1 = (f32[16,3840]{1,0:T(8,128)}, f32[16,3840]{1,0:T(8,128)S(1)}, u32[]{:S(2)}, u32[]{:S(2)}) collective-permute-start(f32[16,3840]{1,0:T(8,128)} %get-tuple-element.91), channel_id=1, source_target_pairs={{0,2},{1,3},{2,0},{3,1},{4,6},{5,7},{6,4},{7,5},{8,10},{9,11},{10,... | collective-permute-start | bytes 737288 | tf_op jit(solution)/shard_map/ppermute | solution.py:274
  91.2 46.6 %collective-permute-start = (f32[16,3840]{1,0:T(8,128)}, f32[16,3840]{1,0:T(8,128)S(1)}, u32[]{:S(2)}, u32[]{:S(2)}) collective-permute-start(f32[16,3840]{1,0:T(8,128)} %get-tuple-element.88), channel_id=1, source_target_pairs={{0,1},{1,0},{2,3},{3,2},{4,5},{5,4},{6,7},{7,6},{8,9},{9,8},{10,11... | collective-permute-start | bytes 737288 | tf_op jit(solution)/shard_map/ppermute | solution.py:274
  105.7 33.3 %collective-permute-start.3 = (f32[16,3840]{1,0:T(8,128)}, f32[16,3840]{1,0:T(8,128)S(1)}, u32[]{:S(2)}, u32[]{:S(2)}) collective-permute-start(f32[16,3840]{1,0:T(8,128)} %get-tuple-element.97), channel_id=1, source_target_pairs={{0,4},{1,5},{2,6},{3,7},{4,0},{5,1},{6,2},{7,3},{8,12},{9,13},{10,... | collective-permute-start | bytes 737288 | tf_op jit(solution)/shard_map/ppermute | solution.py:274
  111.0 29.2 %collective-permute-start.17 = (f32[16,3840]{1,0:T(8,128)}, f32[16,3840]{1,0:T(8,128)S(1)}, u32[]{:S(2)}, u32[]{:S(2)}) collective-permute-start(f32[16,3840]{1,0:T(8,128)} %get-tuple-element.139), channel_id=1, source_target_pairs={{0,18},{1,19},{2,16},{3,17},{4,22},{5,23},{6,20},{7,21},{8,26},{9,... | collective-permute-start | bytes 737288 | tf_op jit(solution)/shard_map/ppermute | solution.py:274
  114.9 26.5 %collective-permute-start.18 = (f32[16,3840]{1,0:T(8,128)}, f32[16,3840]{1,0:T(8,128)S(1)}, u32[]{:S(2)}, u32[]{:S(2)}) collective-permute-start(f32[16,3840]{1,0:T(8,128)} %get-tuple-element.142), channel_id=1, source_target_pairs={{0,19},{1,18},{2,17},{3,16},{4,23},{5,22},{6,21},{7,20},{8,27},{9,... | collective-permute-start | bytes 737288 | tf_op jit(solution)/shard_map/ppermute | solution.py:274
  115.3 26.1 %collective-permute-start.6 = (f32[16,3840]{1,0:T(8,128)}, f32[16,3840]{1,0:T(8,128)S(1)}, u32[]{:S(2)}, u32[]{:S(2)}) collective-permute-start(f32[16,3840]{1,0:T(8,128)} %get-tuple-element.106), channel_id=1, source_target_pairs={{0,7},{1,6},{2,5},{3,4},{4,3},{5,2},{6,1},{7,0},{8,15},{9,14},{10,... | collective-permute-start | bytes 737288 | tf_op jit(solution)/shard_map/ppermute | solution.py:274
  137.7 9.9 %collective-permute-start.5 = (f32[16,3840]{1,0:T(8,128)}, f32[16,3840]{1,0:T(8,128)S(1)}, u32[]{:S(2)}, u32[]{:S(2)}) collective-permute-start(f32[16,3840]{1,0:T(8,128)} %get-tuple-element.103), channel_id=1, source_target_pairs={{0,6},{1,7},{2,4},{3,5},{4,2},{5,3},{6,0},{7,1},{8,14},{9,15},{10,... | collective-permute-start | bytes 737288 | tf_op jit(solution)/shard_map/ppermute | solution.py:274
  139.1 23.7 %collective-permute-start.4 = (f32[16,3840]{1,0:T(8,128)}, f32[16,3840]{1,0:T(8,128)S(1)}, u32[]{:S(2)}, u32[]{:S(2)}) collective-permute-start(f32[16,3840]{1,0:T(8,128)} %get-tuple-element.100), channel_id=1, source_target_pairs={{0,5},{1,4},{2,7},{3,6},{4,1},{5,0},{6,3},{7,2},{8,13},{9,12},{10,... | collective-permute-start | bytes 737288 | tf_op jit(solution)/shard_map/ppermute | solution.py:274
  140.2 22.6 %collective-permute-start.7 = (f32[16,3840]{1,0:T(8,128)}, f32[16,3840]{1,0:T(8,128)S(1)}, u32[]{:S(2)}, u32[]{:S(2)}) collective-permute-start(f32[16,3840]{1,0:T(8,128)} %get-tuple-element.109), channel_id=1, source_target_pairs={{0,8},{1,9},{2,10},{3,11},{4,12},{5,13},{6,14},{7,15},{8,0},{9,1},... | collective-permute-start | bytes 737288 | tf_op jit(solution)/shard_map/ppermute | solution.py:274
  141.4 23.4 %collective-permute-start.19 = (f32[16,3840]{1,0:T(8,128)}, f32[16,3840]{1,0:T(8,128)S(1)}, u32[]{:S(2)}, u32[]{:S(2)}) collective-permute-start(f32[16,3840]{1,0:T(8,128)} %get-tuple-element.145), channel_id=1, source_target_pairs={{0,20},{1,21},{2,22},{3,23},{4,16},{5,17},{6,18},{7,19},{8,28},{9,... | collective-permute-start | bytes 737288 | tf_op jit(solution)/shard_map/ppermute | solution.py:274
  141.4 23.9 %collective-permute-start.20 = (f32[16,3840]{1,0:T(8,128)}, f32[16,3840]{1,0:T(8,128)S(1)}, u32[]{:S(2)}, u32[]{:S(2)}) collective-permute-start(f32[16,3840]{1,0:T(8,128)} %get-tuple-element.148), channel_id=1, source_target_pairs={{0,21},{1,20},{2,23},{3,22},{4,17},{5,16},{6,19},{7,18},{8,29},{9,... | collective-permute-start | bytes 737288 | tf_op jit(solution)/shard_map/ppermute | solution.py:274
  147.6 38.7 %collective-permute-start.10 = (f32[16,3840]{1,0:T(8,128)}, f32[16,3840]{1,0:T(8,128)}, u32[]{:S(2)}, u32[]{:S(2)}) collective-permute-start(f32[16,3840]{1,0:T(8,128)} %get-tuple-element.118), channel_id=1, source_target_pairs={{0,11},{1,10},{2,9},{3,8},{4,15},{5,14},{6,13},{7,12},{8,3},{9,2},... | collective-permute-start | bytes 737288 | tf_op jit(solution)/shard_map/ppermute | solution.py:274
  162.8 25.2 %collective-permute-start.9 = (f32[16,3840]{1,0:T(8,128)}, f32[16,3840]{1,0:T(8,128)}, u32[]{:S(2)}, u32[]{:S(2)}) collective-permute-start(f32[16,3840]{1,0:T(8,128)} %get-tuple-element.115), channel_id=1, source_target_pairs={{0,10},{1,11},{2,8},{3,9},{4,14},{5,15},{6,12},{7,13},{8,2},{9,3},... | collective-permute-start | bytes 737288 | tf_op jit(solution)/shard_map/ppermute | solution.py:274
  162.8 27.7 %collective-permute-start.8 = (f32[16,3840]{1,0:T(8,128)}, f32[16,3840]{1,0:T(8,128)}, u32[]{:S(2)}, u32[]{:S(2)}) collective-permute-start(f32[16,3840]{1,0:T(8,128)} %get-tuple-element.112), channel_id=1, source_target_pairs={{0,9},{1,8},{2,11},{3,10},{4,13},{5,12},{6,15},{7,14},{8,1},{9,0},... | collective-permute-start | bytes 737288 | tf_op jit(solution)/shard_map/ppermute | solution.py:274
  164.9 25.8 %collective-permute-start.11 = (f32[16,3840]{1,0:T(8,128)}, f32[16,3840]{1,0:T(8,128)}, u32[]{:S(2)}, u32[]{:S(2)}) collective-permute-start(f32[16,3840]{1,0:T(8,128)} %get-tuple-element.121), channel_id=1, source_target_pairs={{0,12},{1,13},{2,14},{3,15},{4,8},{5,9},{6,10},{7,11},{8,4},{9,5},... | collective-permute-start | bytes 737288 | tf_op jit(solution)/shard_map/ppermute | solution.py:274
  165.3 29.3 %collective-permute-start.21 = (f32[16,3840]{1,0:T(8,128)}, f32[16,3840]{1,0:T(8,128)}, u32[]{:S(2)}, u32[]{:S(2)}) collective-permute-start(f32[16,3840]{1,0:T(8,128)} %get-tuple-element.151), channel_id=1, source_target_pairs={{0,22},{1,23},{2,20},{3,21},{4,18},{5,19},{6,16},{7,17},{8,30},{9,... | collective-permute-start | bytes 737288 | tf_op jit(solution)/shard_map/ppermute | solution.py:274
  186.4 23.9 %collective-permute-start.22 = (f32[16,3840]{1,0:T(8,128)S(1)}, f32[16,3840]{1,0:T(8,128)S(1)}, u32[]{:S(2)}, u32[]{:S(2)}) collective-permute-start(f32[16,3840]{1,0:T(8,128)S(1)} %copy-done.18), channel_id=1, source_target_pairs={{0,23},{1,22},{2,21},{3,20},{4,19},{5,18},{6,17},{7,16},{8,31},{9,... | collective-permute-start | bytes 737288 | tf_op jit(solution)/shard_map/ppermute | solution.py:274
  188.0 23.5 %collective-permute-start.14 = (f32[16,3840]{1,0:T(8,128)S(1)}, f32[16,3840]{1,0:T(8,128)S(1)}, u32[]{:S(2)}, u32[]{:S(2)}) collective-permute-start(f32[16,3840]{1,0:T(8,128)S(1)} %copy-done.17), channel_id=1, source_target_pairs={{0,15},{1,14},{2,13},{3,12},{4,11},{5,10},{6,9},{7,8},{8,7},{9,6},... | collective-permute-start | bytes 737288 | tf_op jit(solution)/shard_map/ppermute | solution.py:274
  190.5 21.0 %collective-permute-start.13 = (f32[16,3840]{1,0:T(8,128)S(1)}, f32[16,3840]{1,0:T(8,128)S(1)}, u32[]{:S(2)}, u32[]{:S(2)}) collective-permute-start(f32[16,3840]{1,0:T(8,128)S(1)} %copy-done.16), channel_id=1, source_target_pairs={{0,14},{1,15},{2,12},{3,13},{4,10},{5,11},{6,8},{7,9},{8,6},{9,7},... | collective-permute-start | bytes 737288 | tf_op jit(solution)/shard_map/ppermute | solution.py:274
  190.7 22.8 %collective-permute-start.12 = (f32[16,3840]{1,0:T(8,128)S(1)}, f32[16,3840]{1,0:T(8,128)S(1)}, u32[]{:S(2)}, u32[]{:S(2)}) collective-permute-start(f32[16,3840]{1,0:T(8,128)S(1)} %copy-done.14), channel_id=1, source_target_pairs={{0,13},{1,12},{2,15},{3,14},{4,9},{5,8},{6,11},{7,10},{8,5},{9,4},... | collective-permute-start | bytes 737288 | tf_op jit(solution)/shard_map/ppermute | solution.py:274
  194.6 18.9 %collective-permute-start.23 = (f32[16,3840]{1,0:T(8,128)S(1)}, f32[16,3840]{1,0:T(8,128)S(1)}, u32[]{:S(2)}, u32[]{:S(2)}) collective-permute-start(f32[16,3840]{1,0:T(8,128)S(1)} %copy-done.13), channel_id=1, source_target_pairs={{0,24},{1,25},{2,26},{3,27},{4,28},{5,29},{6,30},{7,31},{8,16},{9,... | collective-permute-start | bytes 737288 | tf_op jit(solution)/shard_map/ppermute | solution.py:274
  210.3 50.4 %collective-permute-start.24 = (f32[16,3840]{1,0:T(8,128)S(1)}, f32[16,3840]{1,0:T(8,128)S(1)}, u32[]{:S(2)}, u32[]{:S(2)}) collective-permute-start(f32[16,3840]{1,0:T(8,128)S(1)} %copy-done.11), channel_id=1, source_target_pairs={{0,25},{1,24},{2,27},{3,26},{4,29},{5,28},{6,31},{7,30},{8,17},{9,... | collective-permute-start | bytes 737288 | tf_op jit(solution)/shard_map/ppermute | solution.py:274
  213.5 52.6 %collective-permute-start.29 = (f32[16,3840]{1,0:T(8,128)S(1)}, f32[16,3840]{1,0:T(8,128)S(1)}, u32[]{:S(2)}, u32[]{:S(2)}) collective-permute-start(f32[16,3840]{1,0:T(8,128)S(1)} %copy-done.8), channel_id=1, source_target_pairs={{0,30},{1,31},{2,28},{3,29},{4,26},{5,27},{6,24},{7,25},{8,22},{9,... | collective-permute-start | bytes 737288 | tf_op jit(solution)/shard_map/ppermute | solution.py:274
  215.3 70.2 %collective-permute-start.27 = (f32[16,3840]{1,0:T(8,128)S(1)}, f32[16,3840]{1,0:T(8,128)S(1)}, u32[]{:S(2)}, u32[]{:S(2)}) collective-permute-start(f32[16,3840]{1,0:T(8,128)S(1)} %copy-done.7), channel_id=1, source_target_pairs={{0,28},{1,29},{2,30},{3,31},{4,24},{5,25},{6,26},{7,27},{8,20},{9,... | collective-permute-start | bytes 737288 | tf_op jit(solution)/shard_map/ppermute | solution.py:274
  216.4 69.1 %collective-permute-start.28 = (f32[16,3840]{1,0:T(8,128)S(1)}, f32[16,3840]{1,0:T(8,128)S(1)}, u32[]{:S(2)}, u32[]{:S(2)}) collective-permute-start(f32[16,3840]{1,0:T(8,128)S(1)} %copy-done.6), channel_id=1, source_target_pairs={{0,29},{1,28},{2,31},{3,30},{4,25},{5,24},{6,27},{7,26},{8,21},{9,... | collective-permute-start | bytes 737288 | tf_op jit(solution)/shard_map/ppermute | solution.py:274
  218.3 67.2 %collective-permute-start.26 = (f32[16,3840]{1,0:T(8,128)S(1)}, f32[16,3840]{1,0:T(8,128)S(1)}, u32[]{:S(2)}, u32[]{:S(2)}) collective-permute-start(f32[16,3840]{1,0:T(8,128)S(1)} %copy-done.5), channel_id=1, source_target_pairs={{0,27},{1,26},{2,25},{3,24},{4,31},{5,30},{6,29},{7,28},{8,19},{9,... | collective-permute-start | bytes 737288 | tf_op jit(solution)/shard_map/ppermute | solution.py:274
  260.7 26.3 %collective-permute-start.25 = (f32[16,3840]{1,0:T(8,128)S(1)}, f32[16,3840]{1,0:T(8,128)S(1)}, u32[]{:S(2)}, u32[]{:S(2)}) collective-permute-start(f32[16,3840]{1,0:T(8,128)S(1)} %copy-done.4), channel_id=1, source_target_pairs={{0,26},{1,27},{2,24},{3,25},{4,30},{5,31},{6,28},{7,29},{8,18},{9,... | collective-permute-start | bytes 737288 | tf_op jit(solution)/shard_map/ppermute | solution.py:274
  266.1 26.8 %collective-permute-start.30 = (f32[16,3840]{1,0:T(8,128)S(1)}, f32[16,3840]{1,0:T(8,128)S(1)}, u32[]{:S(2)}, u32[]{:S(2)}) collective-permute-start(f32[16,3840]{1,0:T(8,128)S(1)} %copy-done.3), channel_id=1, source_target_pairs={{0,31},{1,30},{2,29},{3,28},{4,27},{5,26},{6,25},{7,24},{8,23},{9,... | collective-permute-start | bytes 737288 | tf_op jit(solution)/shard_map/ppermute | solution.py:274
  (41 other events, 1117.0 us)
Sparse Core Ops, SparseCore 0:
  17.2 47.0 all-gather.1

commit v3 on v2

--- a/solution.py
+++ b/solution.py
@@ -250,7 +250,8 @@
     )
     targets = jnp.take(targets, device_iota ^ me_flat, axis=0).reshape(fronts, 1, helpers * cap_rows)
 
-    inverse = block_inverse(product(order, head))
+    matrix, targets = lax.optimization_barrier((product(order, head), targets))
+    inverse = block_inverse(matrix)
     active = (own_ids >= PANEL)[:, None]
     current = front_rows[:, :PANEL]
     lower_part = jnp.where(active, product(current, inverse), 0.0)
@@ -262,8 +263,8 @@
     far = [offset for offset in range(devices_all // 2, devices_all)]
     sequence = []
     while near or far:
-        sequence += far[:1] + near[:2]
-        far, near = far[1:], near[2:]
+        sequence += far[:1] + near[:1] + far[1:2] + near[1:3]
+        far, near = far[2:], near[3:]
     arrived = list(outgoing)
     for index, offset in enumerate(sequence):
         pairs = [(device, device ^ offset) for device in range(devices_all)]

time: 318 us -> 323 us (1.016)
  starting transfers between devices: 47.6 us -> 69.9 us
  blocking collectives: 31.4 us -> 10.2 us
  waiting for transfers between devices: 70.7 us -> 76.5 us
    all_to_all x1 -> x0, blocking collectives: 19.7 us -> none  [local(): lax.all_to_all(jnp.take(send_target.astype(jnp.float32).reshape(devices_a...]
    ppermute x31, starting transfers between devices: 47.5 us -> 63.5 us  [local(): arrived[offset] = lax.ppermute(piece, ('front', 'helper'), pairs)]
    all_to_all x0 -> x1, starting transfers between devices: none -> 6.36 us  [local(): lax.all_to_all(jnp.take(send_target.astype(jnp.float32).reshape(devices_a...]
    ppermute x31, waiting for transfers between devices: 70.6 us -> 76.5 us  [local(): arrived[offset] = lax.ppermute(piece, ('front', 'helper'), pairs)]
  transfers between devices with their start and end apart: 32 -> 33, of which waited for: 8 -> 15; matrix products, arithmetic and copies ran while one was open for 6% -> 5% of each run, Pallas kernels for 28% -> 28%
where the time goes in v3:
time: 323 us; the launch traced here: 322 us
  Pallas kernels  123 us (38%)
  waiting for transfers between devices  76.5 us (24%)
  starting transfers between devices  69.9 us (22%)
  between operations  14.6 us (5%)
  matrix products  14.1 us (4%)
  blocking collectives  10.2 us (3%)
  other arithmetic  6.72 us (2%)
  local copies, waits for them, and re-layouts  6.45 us (2%)
    ppermute x31, waiting for transfers between devices, local(): arrived[offset] = lax.ppermute(piece, ('front', 'helper'), pairs)  76.5 us
    ppermute x31, starting transfers between devices, local(): arrived[offset] = lax.ppermute(piece, ('front', 'helper'), pairs)  63.5 us
    pallas_call x4, Pallas kernels, spread_add(): pl.pallas_call(spread_kernel, grid=(parent_width // piece,), out_shape=ja...  61.9 us
    pallas_call x1, Pallas kernels, block_inverse(): pl.pallas_call(inverse_kernel, out_shape=jax.ShapeDtypeStruct((extent, ex...  25.3 us
    pallas_call x1, Pallas kernels, send_rows(): pl.pallas_call(send_kernel, grid=(width // TILE,), out_shape=[jax.ShapeDt...  18.7 us
    pallas_call x1, Pallas kernels, factor_rows(): pl.pallas_call(factor_kernel, grid=(order // TILE,), out_shape=jax.ShapeD...  17.3 us
    dot_general x6, matrix products, product(): jnp.dot(left, right, precision=precision, preferred_element_type=jnp.floa...  14.1 us
    all_gather x1, blocking collectives, local(): lax.all_gather(product(own_slot, front_rows[:, :PANEL]), 'helper', axis=0...  10.2 us
  transfers between devices with their start and end apart: 33, of which 15 were waited for; matrix products, arithmetic and copies ran while one was open for 5% of the time, Pallas kernels for 28%

profile of v3, /device:TPU:9, one launch (start us, length us, event | category | flops | bytes accessed | tf_op | source)
XLA Modules:
  0.0 321.7 jit_solution(12072966836834354658)
XLA Ops:
  9.9 7.2 %fusion = f32[48,3840]{1,0:T(8,128)} fusion(f32[512,4096]{1,0:T(8,128)} %bitcast.45, pred[8,48,512]{2,1,0:T(8,128)(4,1)S(1)} %fusion.4, s32[]{:T(128)S(6)} %select_n.99), kind=kOutput, calls=%fused_computation.3 | convolution fusion | flops 1132462080 | bytes 8626180 | tf_op jit(solution)/shard_map/dot_general | solution.py:17
  17.9 3.1 gather_fusion
  24.3 6.4 %all-to-all-start = ((f32[32,1,16]{2,1,0:T(1,128)}), f32[32,1,16]{2,1,0:T(1,128)S(1)}, u32[]{:S(2)}, u32[]{:S(2)}) async-start(f32[32,1,16]{2,1,0:T(1,128)} %bitcast.8), calls=%async_computation | async-start | bytes 32768 | tf_op jit(solution)/shard_map/all_to_all | solution.py:247
  32.4 10.2 %all_gather.6 = f32[384,256]{1,0:T(8,128)S(1)} all-gather(f32[48,256]{1,0:T(8,128)S(1)} %fusion.7), channel_id=1, replica_groups=mesh['front'=4,'helper'=8] {'helper'}, dimensions={0}, use_global_device_ids=true | all-gather | bytes 442368 | tf_op jit(solution)/shard_map/all_gather | solution.py:229
  44.6 25.3 %panel_inverse.1 = f32[256,256]{1,0:T(8,128)S(1)} custom-call(f32[256,256]{1,0:T(8,128)S(1)} %fusion.10.matrix_ref), custom_call_target="tpu_custom_call" | custom-call | flops 1000000000 | bytes 100000000 | tf_op jit(solution)/shard_map/panel_inverse/pallas_call | solution.py:51
  70.0 2.6 bitcast_select_fusion
  75.2 18.7 %send_rows.1 = (f32[16,3840]{1,0:T(8,128)}, f32[16,3840]{1,0:T(8,128)}, f32[16,3840]{1,0:T(8,128)}, f32[16,3840]{1,0:T(8,128)}, f32[16,3840]{1,0:T(8,128)}, /*in...) custom-call(bf16[512,512]{1,0:T(8,128)(2,1)} %fusion.3.pick_ref, ...), custom_call_target="tpu_custom_call" | custom-call | flops 10000000000 | bytes 30000000 | tf_op jit(solution)/shard_map/send_rows/pallas_call | solution.py:98
  99.3 13.3 %collective-permute-done.3.refs_0_ = f32[16,3840]{1,0:T(8,128)S(1)} collective-permute-done((f32[16,3840]{1,0:T(8,128)}, f32[16,3840]{1,0:T(8,128)S(1)}, u32[]{:S(2)}, u32[]{:S(2)}) %collective-permute-start.3) | collective-permute-done | bytes 245792 | tf_op jit(solution)/shard_map/ppermute | solution.py:275
  112.6 3.4 %collective-permute-start.5 = (f32[16,3840]{1,0:T(8,128)}, f32[16,3840]{1,0:T(8,128)S(1)}, u32[]{:S(2)}, u32[]{:S(2)}) collective-permute-start(f32[16,3840]{1,0:T(8,128)} %get-tuple-element.107), channel_id=1, source_target_pairs={{0,17},{1,16},{2,19},{3,18},{4,21},{5,20},{6,23},{7,22},{8,25},{9,... | collective-permute-start | bytes 737288 | tf_op jit(solution)/shard_map/ppermute | solution.py:275
  116.0 7.1 %collective-permute-done.8.refs_2_ = f32[16,3840]{1,0:T(8,128)S(1)} collective-permute-done((f32[16,3840]{1,0:T(8,128)}, f32[16,3840]{1,0:T(8,128)S(1)}, u32[]{:S(2)}, u32[]{:S(2)}) %collective-permute-start.8) | collective-permute-done | bytes 245792 | tf_op jit(solution)/shard_map/ppermute | solution.py:275
  127.1 3.8 %collective-permute-start.10 = (f32[16,3840]{1,0:T(8,128)}, f32[16,3840]{1,0:T(8,128)S(1)}, u32[]{:S(2)}, u32[]{:S(2)}) collective-permute-start(f32[16,3840]{1,0:T(8,128)} %get-tuple-element.120), channel_id=1, source_target_pairs={{0,19},{1,18},{2,17},{3,16},{4,23},{5,22},{6,21},{7,20},{8,27},{9,... | collective-permute-start | bytes 737288 | tf_op jit(solution)/shard_map/ppermute | solution.py:275
  132.1 2.7 collective-permute-done.4.refs_4_
  134.7 2.5 collective-permute-start.6
  139.6 6.6 %collective-permute-start.15 = (f32[16,3840]{1,0:T(8,128)}, f32[16,3840]{1,0:T(8,128)S(1)}, u32[]{:S(2)}, u32[]{:S(2)}) collective-permute-start(f32[16,3840]{1,0:T(8,128)} %get-tuple-element.133), channel_id=1, source_target_pairs={{0,21},{1,20},{2,23},{3,22},{4,17},{5,16},{6,19},{7,18},{8,29},{9,... | collective-permute-start | bytes 737288 | tf_op jit(solution)/shard_map/ppermute | solution.py:275
  146.1 4.5 %collective-permute-done.7.refs_6_ = f32[16,3840]{1,0:T(8,128)S(1)} collective-permute-done((f32[16,3840]{1,0:T(8,128)}, f32[16,3840]{1,0:T(8,128)S(1)}, u32[]{:S(2)}, u32[]{:S(2)}) %collective-permute-start.7) | collective-permute-done | bytes 245792 | tf_op jit(solution)/shard_map/ppermute | solution.py:275
  150.7 4.5 %collective-permute-start.18 = (f32[16,3840]{1,0:T(8,128)}, f32[16,3840]{1,0:T(8,128)S(1)}, u32[]{:S(2)}, u32[]{:S(2)}) collective-permute-start(f32[16,3840]{1,0:T(8,128)} %get-tuple-element.141), channel_id=1, source_target_pairs={{0,22},{1,23},{2,20},{3,21},{4,18},{5,19},{6,16},{7,17},{8,30},{9,... | collective-permute-start | bytes 737288 | tf_op jit(solution)/shard_map/ppermute | solution.py:275
  155.8 10.6 %collective-permute-done.13.refs_4_ = f32[16,3840]{1,0:T(8,128)S(1)} collective-permute-done((f32[16,3840]{1,0:T(8,128)}, f32[16,3840]{1,0:T(8,128)S(1)}, u32[]{:S(2)}, u32[]{:S(2)}) %collective-permute-start.13) | collective-permute-done | bytes 245792 | tf_op jit(solution)/shard_map/ppermute | solution.py:275
  166.4 2.6 collective-permute-start.11
  171.7 2.9 collective-permute-start.12
  174.6 2.4 collective-permute-done.20.refs_7_
  177.0 3.8 %collective-permute-start.16 = (f32[16,3840]{1,0:T(8,128)}, f32[16,3840]{1,0:T(8,128)S(1)}, u32[]{:S(2)}, u32[]{:S(2)}) collective-permute-start(f32[16,3840]{1,0:T(8,128)} %get-tuple-element.134), channel_id=1, source_target_pairs={{0,11},{1,10},{2,9},{3,8},{4,15},{5,14},{6,13},{7,12},{8,3},{9,2},... | collective-permute-start | bytes 737288 | tf_op jit(solution)/shard_map/ppermute | solution.py:275
  182.2 4.5 %collective-permute-start.21 = (f32[16,3840]{1,0:T(8,128)}, f32[16,3840]{1,0:T(8,128)S(1)}, u32[]{:S(2)}, u32[]{:S(2)}) collective-permute-start(f32[16,3840]{1,0:T(8,128)} %get-tuple-element.147), channel_id=1, source_target_pairs={{0,14},{1,15},{2,12},{3,13},{4,10},{5,11},{6,8},{7,9},{8,6},{9,7},... | collective-permute-start | bytes 737288 | tf_op jit(solution)/shard_map/ppermute | solution.py:275
  186.8 17.3 %factor_rows.1 = f32[512,4096]{1,0:T(8,128)} custom-call(f32[512,256]{1,0:T(8,128)} %get-tuple-element.208.left_ref, f32[512,384]{1,0:T(8,128)} %copy-done.1, f32[512,4096]{1,0:T(8,128)} %bitcast.49, f32[384,3840]{1,0:T(8,128)} %all-gather.2.cloned.1.call-done.tail_ref), custom_call_target="tpu_custom_call" | custom-call | flops 10000000000 | bytes 30000000 | tf_op jit(solution)/shard_map/factor_rows/pallas_call | solution.py:133
  205.1 2.7 collective-permute-start.17
  209.5 5.0 %collective-permute-start.22 = (f32[16,3840]{1,0:T(8,128)S(1)}, f32[16,3840]{1,0:T(8,128)S(1)}, u32[]{:S(2)}, u32[]{:S(2)}) collective-permute-start(f32[16,3840]{1,0:T(8,128)S(1)} %copy-done.11), channel_id=1, source_target_pairs={{0,15},{1,14},{2,13},{3,12},{4,11},{5,10},{6,9},{7,8},{8,7},{9,6},... | collective-permute-start | bytes 737288 | tf_op jit(solution)/shard_map/ppermute | solution.py:275
  214.6 15.5 %spread_add.4.base_ref = f32[256,8192]{1,0:T(8,128)} custom-call(s32[3840]{0:T(1024)} %copy-done, f32[1,128]{1,0:T(1,128)} %get-tuple-element.204.target_ref, f32[256,8192]{1,0:T(8,128)} %base_ref.1, f32[16,3840]{1,0:T(8,128)} %get-tuple-element.90.refs_0_, f32[16,3840]{1,0:T(8,128)} %copy-done.21, f32[16,3840]{1,0:T(8,128)} %copy-done.20, ...), custom_call_target="tpu_custom_call" | custom-call | flops 10000000000 | bytes 50000000 | tf_op jit(solution)/shard_map/spread_add/pallas_call | solution.py:189
  237.4 15.5 %spread_add.5.base_ref = f32[256,8192]{1,0:T(8,128)} custom-call(s32[3840]{0:T(1024)} %get-tuple-element.194.map_ref, f32[1,128]{1,0:T(1,128)} %get-tuple-element.205.target_ref, f32[256,8192]{1,0:T(8,128)} %spread_add.4.base_ref, f32[16,3840]{1,0:T(8,128)} %copy-done.28, f32[16,3840]{1,0:T(8,128)} %copy-done.32, f32[16,3840]{1,0:T(8,128)} %copy-done.29, ...), custom_call_target="tpu_custom_call" | custom-call | flops 10000000000 | bytes 50000000 | tf_op jit(solution)/shard_map/spread_add/pallas_call | solution.py:189
  252.9 18.9 %collective-permute-done.28.refs_5_ = f32[16,3840]{1,0:T(8,128)S(1)} collective-permute-done((f32[16,3840]{1,0:T(8,128)S(1)}, f32[16,3840]{1,0:T(8,128)S(1)}, u32[]{:S(2)}, u32[]{:S(2)}) %collective-permute-start.28) | collective-permute-done | bytes 245792 | tf_op jit(solution)/shard_map/ppermute | solution.py:275
  273.9 15.4 %spread_add.6.base_ref = f32[256,8192]{1,0:T(8,128)} custom-call(s32[3840]{0:T(1024)} %get-tuple-element.197.map_ref, f32[1,128]{1,0:T(1,128)} %get-tuple-element.206.target_ref, f32[256,8192]{1,0:T(8,128)} %spread_add.5.base_ref, f32[16,3840]{1,0:T(8,128)} %copy-done.9, f32[16,3840]{1,0:T(8,128)} %copy-done.12, f32[16,3840]{1,0:T(8,128)} %copy-done.10, ...), custom_call_target="tpu_custom_call" | custom-call | flops 10000000000 | bytes 50000000 | tf_op jit(solution)/shard_map/spread_add/pallas_call | solution.py:189
  289.4 4.0 %collective-permute-done.25.refs_2_ = f32[16,3840]{1,0:T(8,128)S(1)} collective-permute-done((f32[16,3840]{1,0:T(8,128)S(1)}, f32[16,3840]{1,0:T(8,128)S(1)}, u32[]{:S(2)}, u32[]{:S(2)}) %collective-permute-start.25) | collective-permute-done | bytes 245792 | tf_op jit(solution)/shard_map/ppermute | solution.py:275
  293.4 5.4 %collective-permute-done.30.refs_7_ = f32[16,3840]{1,0:T(8,128)S(1)} collective-permute-done((f32[16,3840]{1,0:T(8,128)S(1)}, f32[16,3840]{1,0:T(8,128)S(1)}, u32[]{:S(2)}, u32[]{:S(2)}) %collective-permute-start.30) | collective-permute-done | bytes 245792 | tf_op jit(solution)/shard_map/ppermute | solution.py:275
  299.5 15.4 %spread_add.7 = f32[256,8192]{1,0:T(8,128)} custom-call(s32[3840]{0:T(1024)} %get-tuple-element.195.map_ref, f32[1,128]{1,0:T(1,128)} %get-tuple-element.207.target_ref, f32[256,8192]{1,0:T(8,128)} %spread_add.6.base_ref, f32[16,3840]{1,0:T(8,128)} %copy-done.33, f32[16,3840]{1,0:T(8,128)} %copy-done.30, f32[16,3840]{1,0:T(8,128)} %copy-done.42, ...), custom_call_target="tpu_custom_call" | custom-call | flops 10000000000 | bytes 50000000 | tf_op jit(solution)/shard_map/spread_add/pallas_call | solution.py:189
  (180 shorter events, 43.3 us)
Async XLA Ops:
  7.2 68.0 %all-gather.2.cloned.1.call-start = ((), (), s32[]{:S(2)}) async-start(), calls=%async_computation.1 | async-start | bytes 6635520 | tf_op jit(solution)/shard_map/all_gather | solution.py:230
  24.3 19.7 %all-to-all-start = ((f32[32,1,16]{2,1,0:T(1,128)}), f32[32,1,16]{2,1,0:T(1,128)S(1)}, u32[]{:S(2)}, u32[]{:S(2)}) async-start(f32[32,1,16]{2,1,0:T(1,128)} %bitcast.8), calls=%async_computation | async-start | bytes 32768 | tf_op jit(solution)/shard_map/all_to_all | solution.py:247
  93.9 18.7 %collective-permute-start.3 = (f32[16,3840]{1,0:T(8,128)}, f32[16,3840]{1,0:T(8,128)S(1)}, u32[]{:S(2)}, u32[]{:S(2)}) collective-permute-start(f32[16,3840]{1,0:T(8,128)} %get-tuple-element.102), channel_id=1, source_target_pairs={{0,16},{1,17},{2,18},{3,19},{4,20},{5,21},{6,22},{7,23},{8,24},{9,... | collective-permute-start | bytes 737288 | tf_op jit(solution)/shard_map/ppermute | solution.py:275
  96.1 27.1 %collective-permute-start.8 = (f32[16,3840]{1,0:T(8,128)}, f32[16,3840]{1,0:T(8,128)S(1)}, u32[]{:S(2)}, u32[]{:S(2)}) collective-permute-start(f32[16,3840]{1,0:T(8,128)} %get-tuple-element.115), channel_id=1, source_target_pairs={{0,18},{1,19},{2,16},{3,17},{4,22},{5,23},{6,20},{7,21},{8,26},{9,... | collective-permute-start | bytes 737288 | tf_op jit(solution)/shard_map/ppermute | solution.py:275
  97.0 27.1 %collective-permute-start.1 = (f32[16,3840]{1,0:T(8,128)}, f32[16,3840]{1,0:T(8,128)S(1)}, u32[]{:S(2)}, u32[]{:S(2)}) collective-permute-start(f32[16,3840]{1,0:T(8,128)} %get-tuple-element.95), channel_id=1, source_target_pairs={{0,2},{1,3},{2,0},{3,1},{4,6},{5,7},{6,4},{7,5},{8,10},{9,11},{10,... | collective-permute-start | bytes 737288 | tf_op jit(solution)/shard_map/ppermute | solution.py:275
  97.5 28.4 %collective-permute-start = (f32[16,3840]{1,0:T(8,128)}, f32[16,3840]{1,0:T(8,128)S(1)}, u32[]{:S(2)}, u32[]{:S(2)}) collective-permute-start(f32[16,3840]{1,0:T(8,128)} %get-tuple-element.92), channel_id=1, source_target_pairs={{0,1},{1,0},{2,3},{3,2},{4,5},{5,4},{6,7},{7,6},{8,9},{9,8},{10,11... | collective-permute-start | bytes 737288 | tf_op jit(solution)/shard_map/ppermute | solution.py:275
  98.5 28.6 %collective-permute-start.2 = (f32[16,3840]{1,0:T(8,128)}, f32[16,3840]{1,0:T(8,128)S(1)}, u32[]{:S(2)}, u32[]{:S(2)}) collective-permute-start(f32[16,3840]{1,0:T(8,128)} %get-tuple-element.98), channel_id=1, source_target_pairs={{0,3},{1,2},{2,1},{3,0},{4,7},{5,6},{6,5},{7,4},{8,11},{9,10},{10,... | collective-permute-start | bytes 737288 | tf_op jit(solution)/shard_map/ppermute | solution.py:275
  112.6 18.3 %collective-permute-start.5 = (f32[16,3840]{1,0:T(8,128)}, f32[16,3840]{1,0:T(8,128)S(1)}, u32[]{:S(2)}, u32[]{:S(2)}) collective-permute-start(f32[16,3840]{1,0:T(8,128)} %get-tuple-element.107), channel_id=1, source_target_pairs={{0,17},{1,16},{2,19},{3,18},{4,21},{5,20},{6,23},{7,22},{8,25},{9,... | collective-permute-start | bytes 737288 | tf_op jit(solution)/shard_map/ppermute | solution.py:275
  124.1 15.5 %collective-permute-start.9 = (f32[16,3840]{1,0:T(8,128)}, f32[16,3840]{1,0:T(8,128)S(1)}, u32[]{:S(2)}, u32[]{:S(2)}) collective-permute-start(f32[16,3840]{1,0:T(8,128)} %get-tuple-element.116), channel_id=1, source_target_pairs={{0,7},{1,6},{2,5},{3,4},{4,3},{5,2},{6,1},{7,0},{8,15},{9,14},{10,... | collective-permute-start | bytes 737288 | tf_op jit(solution)/shard_map/ppermute | solution.py:275
  126.0 24.7 %collective-permute-start.7 = (f32[16,3840]{1,0:T(8,128)}, f32[16,3840]{1,0:T(8,128)S(1)}, u32[]{:S(2)}, u32[]{:S(2)}) collective-permute-start(f32[16,3840]{1,0:T(8,128)} %get-tuple-element.111), channel_id=1, source_target_pairs={{0,6},{1,7},{2,4},{3,5},{4,2},{5,3},{6,0},{7,1},{8,14},{9,15},{10,... | collective-permute-start | bytes 737288 | tf_op jit(solution)/shard_map/ppermute | solution.py:275
  127.1 23.5 %collective-permute-start.10 = (f32[16,3840]{1,0:T(8,128)}, f32[16,3840]{1,0:T(8,128)S(1)}, u32[]{:S(2)}, u32[]{:S(2)}) collective-permute-start(f32[16,3840]{1,0:T(8,128)} %get-tuple-element.120), channel_id=1, source_target_pairs={{0,19},{1,18},{2,17},{3,16},{4,23},{5,22},{6,21},{7,20},{8,27},{9,... | collective-permute-start | bytes 737288 | tf_op jit(solution)/shard_map/ppermute | solution.py:275
  130.9 35.5 %collective-permute-start.13 = (f32[16,3840]{1,0:T(8,128)}, f32[16,3840]{1,0:T(8,128)S(1)}, u32[]{:S(2)}, u32[]{:S(2)}) collective-permute-start(f32[16,3840]{1,0:T(8,128)} %get-tuple-element.128), channel_id=1, source_target_pairs={{0,20},{1,21},{2,22},{3,23},{4,16},{5,17},{6,18},{7,19},{8,28},{9,... | collective-permute-start | bytes 737288 | tf_op jit(solution)/shard_map/ppermute | solution.py:275
  134.7 35.6 %collective-permute-start.6 = (f32[16,3840]{1,0:T(8,128)}, f32[16,3840]{1,0:T(8,128)S(1)}, u32[]{:S(2)}, u32[]{:S(2)}) collective-permute-start(f32[16,3840]{1,0:T(8,128)} %get-tuple-element.108), channel_id=1, source_target_pairs={{0,5},{1,4},{2,7},{3,6},{4,1},{5,0},{6,3},{7,2},{8,13},{9,12},{10,... | collective-permute-start | bytes 737288 | tf_op jit(solution)/shard_map/ppermute | solution.py:275
  139.6 32.1 %collective-permute-start.15 = (f32[16,3840]{1,0:T(8,128)}, f32[16,3840]{1,0:T(8,128)S(1)}, u32[]{:S(2)}, u32[]{:S(2)}) collective-permute-start(f32[16,3840]{1,0:T(8,128)} %get-tuple-element.133), channel_id=1, source_target_pairs={{0,21},{1,20},{2,23},{3,22},{4,17},{5,16},{6,19},{7,18},{8,29},{9,... | collective-permute-start | bytes 737288 | tf_op jit(solution)/shard_map/ppermute | solution.py:275
  150.6 26.4 %collective-permute-start.20 = (f32[16,3840]{1,0:T(8,128)}, f32[16,3840]{1,0:T(8,128)S(1)}, u32[]{:S(2)}, u32[]{:S(2)}) collective-permute-start(f32[16,3840]{1,0:T(8,128)} %get-tuple-element.146), channel_id=1, source_target_pairs={{0,23},{1,22},{2,21},{3,20},{4,19},{5,18},{6,17},{7,16},{8,31},{9,... | collective-permute-start | bytes 737288 | tf_op jit(solution)/shard_map/ppermute | solution.py:275
  150.7 31.6 %collective-permute-start.18 = (f32[16,3840]{1,0:T(8,128)}, f32[16,3840]{1,0:T(8,128)S(1)}, u32[]{:S(2)}, u32[]{:S(2)}) collective-permute-start(f32[16,3840]{1,0:T(8,128)} %get-tuple-element.141), channel_id=1, source_target_pairs={{0,22},{1,23},{2,20},{3,21},{4,18},{5,19},{6,16},{7,17},{8,30},{9,... | collective-permute-start | bytes 737288 | tf_op jit(solution)/shard_map/ppermute | solution.py:275
  166.4 37.8 %collective-permute-start.11 = (f32[16,3840]{1,0:T(8,128)}, f32[16,3840]{1,0:T(8,128)S(1)}, u32[]{:S(2)}, u32[]{:S(2)}) collective-permute-start(f32[16,3840]{1,0:T(8,128)} %get-tuple-element.121), channel_id=1, source_target_pairs={{0,8},{1,9},{2,10},{3,11},{4,12},{5,13},{6,14},{7,15},{8,0},{9,1},... | collective-permute-start | bytes 737288 | tf_op jit(solution)/shard_map/ppermute | solution.py:275
  170.3 34.7 %collective-permute-start.14 = (f32[16,3840]{1,0:T(8,128)}, f32[16,3840]{1,0:T(8,128)S(1)}, u32[]{:S(2)}, u32[]{:S(2)}) collective-permute-start(f32[16,3840]{1,0:T(8,128)} %get-tuple-element.129), channel_id=1, source_target_pairs={{0,10},{1,11},{2,8},{3,9},{4,14},{5,15},{6,12},{7,13},{8,2},{9,3},... | collective-permute-start | bytes 737288 | tf_op jit(solution)/shard_map/ppermute | solution.py:275
  171.7 36.1 %collective-permute-start.12 = (f32[16,3840]{1,0:T(8,128)}, f32[16,3840]{1,0:T(8,128)S(1)}, u32[]{:S(2)}, u32[]{:S(2)}) collective-permute-start(f32[16,3840]{1,0:T(8,128)} %get-tuple-element.124), channel_id=1, source_target_pairs={{0,9},{1,8},{2,11},{3,10},{4,13},{5,12},{6,15},{7,14},{8,1},{9,0},... | collective-permute-start | bytes 737288 | tf_op jit(solution)/shard_map/ppermute | solution.py:275
  177.0 30.9 %collective-permute-start.16 = (f32[16,3840]{1,0:T(8,128)}, f32[16,3840]{1,0:T(8,128)S(1)}, u32[]{:S(2)}, u32[]{:S(2)}) collective-permute-start(f32[16,3840]{1,0:T(8,128)} %get-tuple-element.134), channel_id=1, source_target_pairs={{0,11},{1,10},{2,9},{3,8},{4,15},{5,14},{6,13},{7,12},{8,3},{9,2},... | collective-permute-start | bytes 737288 | tf_op jit(solution)/shard_map/ppermute | solution.py:275
  182.2 27.3 %collective-permute-start.21 = (f32[16,3840]{1,0:T(8,128)}, f32[16,3840]{1,0:T(8,128)S(1)}, u32[]{:S(2)}, u32[]{:S(2)}) collective-permute-start(f32[16,3840]{1,0:T(8,128)} %get-tuple-element.147), channel_id=1, source_target_pairs={{0,14},{1,15},{2,12},{3,13},{4,10},{5,11},{6,8},{7,9},{8,6},{9,7},... | collective-permute-start | bytes 737288 | tf_op jit(solution)/shard_map/ppermute | solution.py:275
  204.2 26.0 %collective-permute-start.19 = (f32[16,3840]{1,0:T(8,128)S(1)}, f32[16,3840]{1,0:T(8,128)S(1)}, u32[]{:S(2)}, u32[]{:S(2)}) collective-permute-start(f32[16,3840]{1,0:T(8,128)S(1)} %copy-done.16), channel_id=1, source_target_pairs={{0,13},{1,12},{2,15},{3,14},{4,9},{5,8},{6,11},{7,10},{8,5},{9,4},... | collective-permute-start | bytes 737288 | tf_op jit(solution)/shard_map/ppermute | solution.py:275
  205.1 25.6 %collective-permute-start.17 = (f32[16,3840]{1,0:T(8,128)S(1)}, f32[16,3840]{1,0:T(8,128)S(1)}, u32[]{:S(2)}, u32[]{:S(2)}) collective-permute-start(f32[16,3840]{1,0:T(8,128)S(1)} %copy-done.15), channel_id=1, source_target_pairs={{0,12},{1,13},{2,14},{3,15},{4,8},{5,9},{6,10},{7,11},{8,4},{9,5},... | collective-permute-start | bytes 737288 | tf_op jit(solution)/shard_map/ppermute | solution.py:275
  207.8 22.9 %collective-permute-start.24 = (f32[16,3840]{1,0:T(8,128)S(1)}, f32[16,3840]{1,0:T(8,128)S(1)}, u32[]{:S(2)}, u32[]{:S(2)}) collective-permute-start(f32[16,3840]{1,0:T(8,128)S(1)} %copy-done.14), channel_id=1, source_target_pairs={{0,25},{1,24},{2,27},{3,26},{4,29},{5,28},{6,31},{7,30},{8,17},{9,... | collective-permute-start | bytes 737288 | tf_op jit(solution)/shard_map/ppermute | solution.py:275
  207.9 24.1 %collective-permute-start.23 = (f32[16,3840]{1,0:T(8,128)S(1)}, f32[16,3840]{1,0:T(8,128)S(1)}, u32[]{:S(2)}, u32[]{:S(2)}) collective-permute-start(f32[16,3840]{1,0:T(8,128)S(1)} %copy-done.13), channel_id=1, source_target_pairs={{0,24},{1,25},{2,26},{3,27},{4,28},{5,29},{6,30},{7,31},{8,16},{9,... | collective-permute-start | bytes 737288 | tf_op jit(solution)/shard_map/ppermute | solution.py:275
  209.5 27.0 %collective-permute-start.22 = (f32[16,3840]{1,0:T(8,128)S(1)}, f32[16,3840]{1,0:T(8,128)S(1)}, u32[]{:S(2)}, u32[]{:S(2)}) collective-permute-start(f32[16,3840]{1,0:T(8,128)S(1)} %copy-done.11), channel_id=1, source_target_pairs={{0,15},{1,14},{2,13},{3,12},{4,11},{5,10},{6,9},{7,8},{8,7},{9,6},... | collective-permute-start | bytes 737288 | tf_op jit(solution)/shard_map/ppermute | solution.py:275
  230.7 41.1 %collective-permute-start.28 = (f32[16,3840]{1,0:T(8,128)S(1)}, f32[16,3840]{1,0:T(8,128)S(1)}, u32[]{:S(2)}, u32[]{:S(2)}) collective-permute-start(f32[16,3840]{1,0:T(8,128)S(1)} %copy-done.8), channel_id=1, source_target_pairs={{0,29},{1,28},{2,31},{3,30},{4,25},{5,24},{6,27},{7,26},{8,21},{9,... | collective-permute-start | bytes 737288 | tf_op jit(solution)/shard_map/ppermute | solution.py:275
  232.0 57.3 %collective-permute-start.26 = (f32[16,3840]{1,0:T(8,128)S(1)}, f32[16,3840]{1,0:T(8,128)S(1)}, u32[]{:S(2)}, u32[]{:S(2)}) collective-permute-start(f32[16,3840]{1,0:T(8,128)S(1)} %copy-done.7), channel_id=1, source_target_pairs={{0,27},{1,26},{2,25},{3,24},{4,31},{5,30},{6,29},{7,28},{8,19},{9,... | collective-permute-start | bytes 737288 | tf_op jit(solution)/shard_map/ppermute | solution.py:275
  233.5 55.9 %collective-permute-start.29 = (f32[16,3840]{1,0:T(8,128)S(1)}, f32[16,3840]{1,0:T(8,128)S(1)}, u32[]{:S(2)}, u32[]{:S(2)}) collective-permute-start(f32[16,3840]{1,0:T(8,128)S(1)} %copy-done.6), channel_id=1, source_target_pairs={{0,30},{1,31},{2,28},{3,29},{4,26},{5,27},{6,24},{7,25},{8,22},{9,... | collective-permute-start | bytes 737288 | tf_op jit(solution)/shard_map/ppermute | solution.py:275
  234.9 54.5 %collective-permute-start.27 = (f32[16,3840]{1,0:T(8,128)S(1)}, f32[16,3840]{1,0:T(8,128)S(1)}, u32[]{:S(2)}, u32[]{:S(2)}) collective-permute-start(f32[16,3840]{1,0:T(8,128)S(1)} %copy-done.5), channel_id=1, source_target_pairs={{0,28},{1,29},{2,30},{3,31},{4,24},{5,25},{6,26},{7,27},{8,20},{9,... | collective-permute-start | bytes 737288 | tf_op jit(solution)/shard_map/ppermute | solution.py:275
  236.5 56.9 %collective-permute-start.25 = (f32[16,3840]{1,0:T(8,128)S(1)}, f32[16,3840]{1,0:T(8,128)S(1)}, u32[]{:S(2)}, u32[]{:S(2)}) collective-permute-start(f32[16,3840]{1,0:T(8,128)S(1)} %copy-done.4), channel_id=1, source_target_pairs={{0,26},{1,27},{2,24},{3,25},{4,30},{5,31},{6,28},{7,29},{8,18},{9,... | collective-permute-start | bytes 737288 | tf_op jit(solution)/shard_map/ppermute | solution.py:275
  271.8 27.0 %collective-permute-start.30 = (f32[16,3840]{1,0:T(8,128)S(1)}, f32[16,3840]{1,0:T(8,128)S(1)}, u32[]{:S(2)}, u32[]{:S(2)}) collective-permute-start(f32[16,3840]{1,0:T(8,128)S(1)} %copy-done.3), channel_id=1, source_target_pairs={{0,31},{1,30},{2,29},{3,28},{4,27},{5,26},{6,25},{7,24},{8,23},{9,... | collective-permute-start | bytes 737288 | tf_op jit(solution)/shard_map/ppermute | solution.py:275
  (46 other events, 1029.1 us)
Sparse Core Ops, SparseCore 0:
  17.2 46.1 all-gather.1
